TPU v7x, 512 devices: a whole 4x8x8 slice. The times are simulated.
512 devices in a mesh: replica: 32 (over y, z_hi), mp: 16 (over z_lo, x, core).
Axes of the slice: x: 4, y: 8, z: 8 (z_hi: 4, z_lo: 2; z = z_hi * 2 + z_lo), core: 2. Of those that a mesh axis runs over, the one named last changes fastest.
Arguments:
- inputs: bfloat16 [32, 384, 4608], P('replica', 'mp'), may hold values from -10 to 10
- out_grads: bfloat16 [32, 384, 4608], P('replica', 'mp'), may hold values from -6 to 6
- norm_gain: float32 [4608], replicated, may hold values from 0.5 to 1.5
- doc_ids: int32 [32, 384], P('replica'), may hold values from 0 to 3, never falling along the last dimension, each value on 1 to 192 neighbouring positions
- w_query: bfloat16 [32, 4608, 2048], P('replica', None, 'mp'), may hold values from -9 to 9
- w_keyval: bfloat16 [32, 4608, 2048], P('replica', None, 'mp'), may hold values from -9 to 9
- w_out: bfloat16 [32, 2048, 4608], P('replica', 'mp'), may hold values from -6 to 6
- outer_params: float32 [16, 128, 4608], P('mp', 'replica'), may hold values from -6 to 6
- outer_moment: float32 [16, 128, 4608], P('mp', 'replica'), may hold values from -6 to 6
Outputs:
- input_grads: bfloat16 [32, 384, 4608], P('replica', 'mp')
- new_params: float32 [16, 128, 4608], P('mp', 'replica')
- new_moment: float32 [16, 128, 4608], P('mp', 'replica')
All inputs are finite; a program needn't handle non-finite values.
Results may differ from a plain program's by a relative error of at most 0.018.
Values may be sent and summed in bfloat16 or wider, within the bound.
A program may use at most 64 MiB of HBM per device.

v0:
```python
import jax
import jax.numpy as jnp
from jax import lax
from jax.sharding import PartitionSpec as P

D = 4608
HEAD_DIM = 128


def swapped(x, axis, distance):
    return lax.ppermute(x, axis, [(i, i ^ 1 << distance) for i in range(lax.axis_size(axis))])


def on_device(
    inputs, out_grads, norm_gain, doc_ids, w_query, w_keyval, w_out, outer_params, outer_moment
):
    width_scale = D ** (-0.5)
    score_scale = 144.0 ** (-0.5)
    model_size = lax.axis_size("mp")
    out_scale = (model_size * HEAD_DIM) ** (-0.5)
    inputs_float = inputs[0].astype(jnp.float32)
    inv_rms = lax.rsqrt(jnp.mean(inputs_float * inputs_float, axis=-1, keepdims=True) + 1e-06)
    normed = (inputs_float * inv_rms * norm_gain).astype(jnp.bfloat16)
    all_normed, all_grads = (
        lax.all_gather(normed, "mp", axis=0, tiled=True),
        lax.all_gather(out_grads[0], "mp", axis=0, tiled=True),
    )
    query_weight = w_query[0]
    keyval_weight = w_keyval[0]
    queries = (
        jnp.dot(all_normed, query_weight, preferred_element_type=jnp.float32) * width_scale
    ).astype(jnp.bfloat16)
    projected = (
        jnp.dot(all_normed, keyval_weight, preferred_element_type=jnp.float32) * width_scale
    ).astype(jnp.bfloat16)
    partner = swapped(projected, "mp", 0)
    is_even = lax.axis_index("mp") % 2 == 0
    keys_head = jnp.where(is_even, projected, partner)
    values_head = jnp.where(is_even, partner, projected)
    seq_len = all_normed.shape[0]
    positions = jnp.arange(seq_len)
    documents = doc_ids[0]
    allowed_pairs = (positions[None, :] <= positions[:, None]) & (
        documents[:, None] == documents[None, :]
    )
    contract_last = (((1,), (1,)), ((), ()))
    contract_first = (((0,), (0,)), ((), ()))
    scores = (
        lax.dot_general(queries, keys_head, contract_last, preferred_element_type=jnp.float32)
        * score_scale
    )
    scores = jnp.where(allowed_pairs, scores, -1e30)
    probs = jax.nn.softmax(scores, axis=-1)
    probs_low = probs.astype(jnp.bfloat16)
    head_grads = lax.dot_general(
        all_grads, w_out[0], contract_last, preferred_element_type=jnp.float32
    )
    head_grads = (head_grads * out_scale).astype(jnp.bfloat16)
    prob_grads = lax.dot_general(
        head_grads, values_head, contract_last, preferred_element_type=jnp.float32
    )
    score_grads = (
        probs * (prob_grads - jnp.sum(probs * prob_grads, axis=-1, keepdims=True)) * score_scale
    )
    score_grads = score_grads.astype(jnp.bfloat16)
    query_grads = jnp.dot(score_grads, keys_head, preferred_element_type=jnp.float32).astype(
        jnp.bfloat16
    )
    key_part = lax.dot_general(
        score_grads, queries, contract_first, preferred_element_type=jnp.float32
    ).astype(jnp.bfloat16)
    value_part = lax.dot_general(
        probs_low, head_grads, contract_first, preferred_element_type=jnp.float32
    ).astype(jnp.bfloat16)
    outgoing = jnp.where(is_even, value_part, key_part)
    own_piece = jnp.where(is_even, key_part, value_part)
    received = swapped(outgoing, "mp", 0)
    keyval_grads = (own_piece.astype(jnp.float32) + received.astype(jnp.float32)).astype(
        jnp.bfloat16
    )
    term = lax.dot_general(
        query_grads, query_weight, contract_last, preferred_element_type=jnp.float32
    )
    term = term + lax.dot_general(
        keyval_grads, keyval_weight, contract_last, preferred_element_type=jnp.float32
    )
    normed_grads = lax.psum_scatter(
        (term * width_scale).astype(jnp.bfloat16), "mp", scatter_dimension=0, tiled=True
    ).astype(jnp.float32)
    scaled = normed_grads * norm_gain
    centered = inputs_float * inv_rms
    result = out_grads[0].astype(jnp.float32) + inv_rms * (
        scaled - centered * jnp.mean(scaled * centered, axis=-1, keepdims=True)
    )
    input_grads = result.astype(jnp.bfloat16)[None]
    replica_count = lax.axis_size("replica")
    mine = lax.psum_scatter(
        w_out[0].astype(jnp.float32).astype(jnp.bfloat16),
        "replica",
        scatter_dimension=0,
        tiled=True,
    ).astype(jnp.float32)
    local_mean = mine / replica_count
    delta = outer_params[0] - local_mean
    new_moment = 0.9 * outer_moment[0] + delta
    new_params = outer_params[0] - 0.7 * (delta + 0.9 * new_moment)
    return (input_grads, new_params[None], new_moment[None])


def solution(mesh):
    placed = (
        P("replica", "mp", None),
        P("replica", "mp", None),
        P(),
        P("replica", None),
        P("replica", None, "mp"),
        P("replica", None, "mp"),
        P("replica", "mp", None),
        P("mp", "replica", None),
        P("mp", "replica", None),
    )
    return jax.shard_map(
        on_device,
        mesh=mesh,
        in_specs=placed,
        out_specs=(P("replica", "mp", None), P("mp", "replica", None), P("mp", "replica", None)),
        check_vma=False,
    )
```

profile of v0, /device:TPU:8, one launch (start us, length us, event | category | flops | bytes accessed | tf_op | source)
XLA Modules:
  0.0 506.0 jit_solution(13711823419353073176)
XLA Ops:
  7.2 0.0 copy-start
  7.2 0.0 copy-start.3
  7.2 0.0 all-gather.4.cloned.1.call-start
  7.2 1.2 fusion.42
  8.5 1.8 fusion.36
  10.2 0.0 all-gather.4.cloned.1.call-update
  10.3 0.0 all-gather.6.cloned.1.call-start
  10.3 0.7 all-gather.6.cloned.1.call-update
  11.0 0.7 reduce
  11.7 45.6 %all-gather.4.cloned.1.call-done = bf16[384,4608]{1,0:T(8,128)(2,1)} async-done(((bf16[24,4608]{1,0:T(8,128)(2,1)}), bf16[384,4608]{1,0:T(8,128)(2,1)}) %all-gather.4.cloned.1.call-update) | async-done | bytes 3538960 | tf_op jit(solution)/shard_map/all_gather | solution.py:25
  57.3 3.4 fusion.24
  60.8 2.1 collective-permute-start
  62.9 38.3 %all-gather.6.cloned.1.call-done = bf16[1,384,4608]{2,1,0:T(8,128)(2,1)} async-done(((bf16[1,24,4608]{2,1,0:T(8,128)(2,1)}), bf16[1,384,4608]{2,1,0:T(8,128)(2,1)}) %all-gather.6.cloned.1.call-update) | async-done | bytes 3538960 | tf_op jit(solution)/shard_map/all_gather | solution.py:26
  101.2 0.0 copy-done.3
  101.2 3.1 fusion.21
  104.3 0.0 all-reduce.3.cloned.1.call-start
  104.4 0.7 all-reduce.3.cloned.1.call-update
  105.0 0.0 reduce-scatter.2.cloned.1.call-start
  105.1 0.0 copy-done
  105.1 3.1 fusion.27
  108.2 0.0 collective-permute-done
  108.2 0.3 fusion.54
  108.5 0.1 fusion.35
  108.6 0.3 multiply_reduce_fusion
  108.9 0.2 multiply_convert_fusion
  109.0 0.2 convolution_convert_fusion.1
  109.3 0.2 broadcast_select_fusion
  109.5 0.0 copy-start.1
  109.6 2.3 collective-permute-start.1
  111.8 4.2 fusion.8
  116.1 0.0 collective-permute-done.1
  116.1 0.0 copy-done.1
  116.1 5.9 %fusion.1 = bf16[384,4608]{1,0:T(8,128)(2,1)} fusion(f32[384,4608]{1,0:T(8,128)} %fusion.8, bf16[1,4608,128]{2,1,0:T(8,128)(2,1)S(1)} %copy-done.1, bf16[384,128]{1,0:T(8,128)(2,1)S(1)} %collective-permute-done.1, bf16[384,128]{1,0:T(8,128)(2,1)S(1)} %convolution_convert_fusion.1, bf16[384,128]{1,0:T(8,128)(2,1)S(1)} %get-tuple-element.10, pred[]{:T(512)S(6)} %eq.24), kind=kOutput, calls=%fused_computation.2 | convolution fusion | flops 458539008 | bytes 12091393 | tf_op jit(solution)/shard_map/dot_general | solution.py:84
  122.0 0.0 copy-start.6
  122.0 0.0 copy-start.7
  122.0 0.0 copy-start.2
  122.0 0.0 copy-start.5
  122.0 0.0 copy-start.4
  122.0 0.0 reduce-scatter.2.cloned.1.call-update
  122.0 1.4 dynamic-slice
  124.0 301.4 %all-reduce.3.cloned.1.call-done = bf16[128,4608]{1,0:T(8,128)(2,1)} async-done(((bf16[128,4608]{1,0:T(8,128)(2,1)}), bf16[128,4608]{1,0:T(8,128)(2,1)}) %all-reduce.3.cloned.1.call-update) | async-done | bytes 1179664
  425.5 0.0 copy-done.6
  425.5 0.0 copy-done.7
  425.5 1.6 fusion.51
  427.1 69.4 %reduce-scatter.2.cloned.1.call-done = bf16[24,4608]{1,0:T(8,128)(2,1)} async-done(((bf16[384,4608]{1,0:T(8,128)(2,1)}), bf16[24,4608]{1,0:T(8,128)(2,1)}) %reduce-scatter.2.cloned.1.call-update) | async-done | bytes 221200 | tf_op jit(solution)/shard_map/reduce_scatter | solution.py:87
  496.4 0.0 copy-done.2
  496.5 0.0 copy-done.5
  496.5 1.2 fusion.37
  497.6 0.0 copy-done.4
  497.6 1.8 fusion.44
  (2 shorter events, 0.0 us)
Async XLA Ops:
  7.2 97.9 %copy-start = (bf16[1,4608,128]{2,1,0:T(8,128)(2,1)S(1)}, bf16[1,4608,128]{2,1,0:T(8,128)(2,1)}, u32[]{:S(2)}) copy-start(bf16[1,4608,128]{2,1,0:T(8,128)(2,1)} %param.13) | copy-start | bytes 3538948
  7.2 94.1 %copy-start.3 = (bf16[1,128,4608]{2,1,0:T(8,128)(2,1)S(1)}, bf16[1,128,4608]{2,1,0:T(8,128)(2,1)}, u32[]{:S(2)}) copy-start(bf16[1,128,4608]{2,1,0:T(8,128)(2,1)} %param.15) | copy-start | bytes 3538948
  7.2 50.2 %all-gather.4.cloned.1.call-start = ((), (), s32[]{:S(2)}) async-start(), calls=%async_computation.1 | async-start | bytes 3760128 | tf_op jit(solution)/shard_map/all_gather | solution.py:25
  10.3 91.0 %all-gather.6.cloned.1.call-start = ((), (), s32[]{:S(2)}) async-start(), calls=%async_computation.3 | async-start | bytes 3760128 | tf_op jit(solution)/shard_map/all_gather | solution.py:26
  60.8 47.4 %collective-permute-start = (bf16[384,128]{1,0:T(8,128)(2,1)S(1)}, bf16[384,128]{1,0:T(8,128)(2,1)S(1)}, u32[]{:S(2)}, u32[]{:S(2)}) collective-permute-start(bf16[384,128]{1,0:T(8,128)(2,1)S(1)} %fusion.24), channel_id=1, source_target_pairs={{0,1},{1,0},{2,3},{3,2},{4,5},{5,4},{6,7},{7,6},{8,9},{9,8},{10,11... | collective-permute-start | bytes 294920 | tf_op jit(solution)/shard_map/ppermute | solution.py:11
  104.3 321.2 %all-reduce.3.cloned.1.call-start = ((), (), s32[]{:S(2)}) async-start(), calls=%async_computation.4 | async-start | bytes 2359296
  105.0 391.4 %reduce-scatter.2.cloned.1.call-start = ((), (), s32[]{:S(2)}) async-start(), calls=%async_computation.2 | async-start | bytes 3760128 | tf_op jit(solution)/shard_map/reduce_scatter | solution.py:87
  109.5 6.5 %copy-start.1 = (bf16[1,4608,128]{2,1,0:T(8,128)(2,1)S(1)}, bf16[1,4608,128]{2,1,0:T(8,128)(2,1)}, u32[]{:S(2)}) copy-start(bf16[1,4608,128]{2,1,0:T(8,128)(2,1)} %param.14) | copy-start | bytes 3538948
  109.6 6.5 %collective-permute-start.1 = (bf16[384,128]{1,0:T(8,128)(2,1)S(1)}, bf16[384,128]{1,0:T(8,128)(2,1)S(1)}, u32[]{:S(2)}, u32[]{:S(2)}) collective-permute-start(bf16[384,128]{1,0:T(8,128)(2,1)S(1)} %get-tuple-element.9), channel_id=1, source_target_pairs={{0,1},{1,0},{2,3},{3,2},{4,5},{5,4},{6,7},{7,6},{8,9},{9,8},{10,11... | collective-permute-start | bytes 294920 | tf_op jit(solution)/shard_map/ppermute | solution.py:11
  122.0 303.5 %copy-start.6 = (f32[1,4,4608]{2,1,0:T(4,128)S(1)}, f32[1,4,4608]{2,1,0:T(4,128)}, u32[]{:S(2)}) copy-start(f32[1,4,4608]{2,1,0:T(4,128)} %param.16) | copy-start | bytes 221188
  122.0 303.5 %copy-start.7 = (f32[1,4,4608]{2,1,0:T(4,128)S(1)}, f32[1,4,4608]{2,1,0:T(4,128)}, u32[]{:S(2)}) copy-start(f32[1,4,4608]{2,1,0:T(4,128)} %param.17) | copy-start | bytes 221188
  122.0 374.5 %copy-start.2 = (bf16[1,24,4608]{2,1,0:T(8,128)(2,1)S(1)}, bf16[1,24,4608]{2,1,0:T(8,128)(2,1)}, u32[]{:S(2)}) copy-start(bf16[1,24,4608]{2,1,0:T(8,128)(2,1)} %param.9) | copy-start | bytes 663556
  122.0 374.5 %copy-start.5 = (f32[4608]{0:T(1024)S(1)}, f32[4608]{0:T(1024)}, u32[]{:S(2)}) copy-start(f32[4608]{0:T(1024)} %param.11) | copy-start | bytes 55300
  122.0 375.6 %copy-start.4 = (bf16[1,24,4608]{2,1,0:T(8,128)(2,1)S(1)}, bf16[1,24,4608]{2,1,0:T(8,128)(2,1)}, u32[]{:S(2)}) copy-start(bf16[1,24,4608]{2,1,0:T(8,128)(2,1)} %param.10) | copy-start | bytes 663556
Sparse Core Ops, SparseCore 0:
  10.7 46.5 all-gather.3
  59.5 41.7 all-gather.5
  108.1 317.3 all-reduce.2
  428.4 67.9 reduce-scatter.1
where the time goes:
time: 507 us; the launch traced here: 506 us
  waiting for transfers between devices  456 us (90%)
  matrix products  20.7 us (4%)
  between operations  14.6 us (3%)
  other arithmetic  8.57 us (2%)
    unnamed x5, waiting for transfers between devices  303 us
    reduce_scatter x1, waiting for transfers between devices, on_device(): lax.psum_scatter((term * width_scale).astype(jnp.bfloat16), 'mp', scatter...  69.4 us
    all_gather x1, waiting for transfers between devices, on_device(): lax.all_gather(normed, 'mp', axis=0, tiled=True)  45.6 us
    all_gather x1, waiting for transfers between devices, on_device(): lax.all_gather(out_grads[0], 'mp', axis=0, tiled=True)  38.3 us
  transfers between devices with their start and end apart: 6, of which 4 were waited for; matrix products, arithmetic and copies ran while one was open for 5% of the time, Pallas kernels for 0%

commit v1 on v0

v1 whole, which is shorter than its diff:
```python
import jax
import jax.numpy as jnp
from jax import lax
from jax.experimental import pallas as pl
from jax.experimental.pallas import tpu as pltpu
from jax.sharding import PartitionSpec as P

D = 4608
HEAD_DIM = 128
SEQ = 384
ROWS = 24
HALF = 192
GATHER = 6
GW = D // GATHER
SUMS = 9
SW = D // SUMS
Y_SIZE = 8
Z_HI = 4
OUTER_ROWS = 4
N_REPLICA = 32
MESH = pl.DeviceIdType.MESH
F32 = jnp.float32
BF16 = jnp.bfloat16
CONTRACT_LAST = (((1,), (1,)), ((), ()))
CONTRACT_FIRST = (((0,), (0,)), ((), ()))
MAX_SENDS = 192
SUM_PLAN = (
    ("z", 1), ("x", 0), ("z", 1), ("x", 1), ("z", 1), ("x", 0), ("z", 0), ("x", 1), ("x", 0),
)


def kernel(
    inputs, out_grads, gain, docs, w_query, w_keyval, w_out, outer_params, outer_moment,
    input_grads, new_params, new_moment,
    normed_all, grads_all, w_in, w_back, bias, acc_in, acc_back, heads, heads_out,
    back, back_out, back_in, grad_rows, terms, hop_x, near_x, hop_z, near_z, from_z_x, from_z_z,
    totals, relay, far, y_in, z_out, z_in, send_sems, recv_sems, local_sems,
):
    width_scale = D ** (-0.5)
    score_scale = 144.0 ** (-0.5)
    out_scale = (16 * HEAD_DIM) ** (-0.5)
    replica = lax.axis_index("replica")
    model = lax.axis_index("mp")
    c = lax.rem(model, 2)
    x = lax.rem(lax.div(model, 2), 4)
    z = lax.div(model, 8)
    y = lax.div(replica, Z_HI)
    zh = lax.rem(replica, Z_HI)
    other_c = 1 - c
    other_z = 1 - z
    x_at = [lax.rem(x + i, 4) for i in range(4)]

    def on_model(zz, xx, cc):
        return (replica, (zz * 4 + xx) * 2 + cc)

    right = on_model(z, x_at[1], c)
    left = on_model(z, x_at[3], c)
    across = on_model(other_z, x, c)
    sibling = on_model(z, x, other_c)
    sides = (right, left)

    def y_device(distance):
        return (lax.rem(y + distance + Y_SIZE, Y_SIZE) * Z_HI + zh, model)

    def z_device(distance):
        return (y * Z_HI + lax.rem(zh + distance, Z_HI), model)

    partners = [right, left, across, sibling]
    partners += [y_device(d) for d in (1, -1, 2, -2, 3, -3)]
    partners += [z_device(d) for d in (1, 2, 3)]
    barrier = pltpu.get_barrier_semaphore()
    for partner in partners:
        pl.semaphore_signal(barrier, inc=1, device_id=partner, device_id_type=MESH)

    sent = []

    def send(src, dst, device):
        index = len(sent)
        assert index < MAX_SENDS
        copy = pltpu.make_async_remote_copy(
            src_ref=src, dst_ref=dst, send_sem=send_sems.at[index], recv_sem=recv_sems.at[index],
            device_id=device, device_id_type=MESH,
        )
        copy.start()
        sent.append(copy)
        return copy

    own_columns = pl.ds(pl.multiple_of(c * HEAD_DIM, HEAD_DIM), HEAD_DIM)
    own_keyval = pl.ds(pl.multiple_of(2 * HEAD_DIM + c * HEAD_DIM, HEAD_DIM), HEAD_DIM)
    weight_moves = (
        (w_out, w_back.at[own_columns, :]),
        (w_query, w_in.at[:, own_columns]),
        (w_keyval, w_in.at[:, own_keyval]),
    )
    local = []
    for index, (src, dst) in enumerate(weight_moves):
        copy = pltpu.make_async_copy(src, dst, local_sems.at[index])
        copy.start()
        local.append(copy)

    rows = inputs[...].astype(F32)
    inv_rms = lax.rsqrt(jnp.sum(rows * rows, axis=-1, keepdims=True) * (1.0 / D) + 1e-06)
    normed_all[z, x] = (rows * inv_rms * gain[...]).astype(BF16)
    grads_all[z, x] = out_grads[...]

    pl.semaphore_wait(barrier, len(partners))

    def columns(k):
        return pl.ds(k * GW, GW)

    def normed_part(zz, xx, k):
        return normed_all.at[zz, xx, :, columns(k)]

    def grads_part(zz, xx, k):
        return grads_all.at[zz, xx, :, columns(k)]

    chunks = range(GATHER)
    grads_across, normed_near, normed_across = [], [], []
    for k in chunks:
        part = grads_part(z, x, k)
        grads_across.append(send(part, part, across))
        part = normed_part(z, x, k)
        normed_near.append([send(part, part, side) for side in sides])
    for k in chunks:
        part = normed_part(z, x, k)
        normed_across.append([send(part, part, across)])

    def y_rows(distance, base=0):
        owner = lax.rem(y + distance + Y_SIZE, Y_SIZE)
        return pl.ds(pl.multiple_of(base + owner * 16, 16), 16)

    half_columns = (pl.ds(0, D // 2), pl.ds(D // 2, D // 2))
    relays = []
    for i, distance in enumerate((1, -1)):
        relays.append(
            send(w_out.at[y_rows(4), half_columns[i]], relay.at[i], y_device(distance))
        )
    weights = [send(src, dst, sibling) for src, dst in weight_moves]
    y_moves = []
    for i, distance in enumerate((1, -1, 2, -2)):
        y_moves.append(send(w_out.at[y_rows(distance), :], y_in.at[i], y_device(distance)))

    row_at = lax.broadcasted_iota(jnp.int32, (SEQ, SEQ), 0)
    column_at = lax.broadcasted_iota(jnp.int32, (SEQ, SEQ), 1)
    documents = jnp.broadcast_to(docs[...].astype(F32), (SEQ, SEQ))
    own_document = jnp.sum(
        jnp.where(row_at == column_at, documents, 0.0), axis=-1, keepdims=True
    )
    allowed = (column_at <= row_at) & (documents == own_document)
    bias[...] = jnp.where(allowed, 0.0, -1e30)

    normed_far, grads_near = [], []
    for k in chunks:
        for i, (side, slot) in enumerate(((right, 3), (left, 1))):
            normed_near[k][i].wait_recv()
            part = normed_part(z, x_at[slot], k)
            if k % 2 == i:
                normed_far.append(send(part, part, side))
            normed_across[k].append(send(part, part, across))
        grads_across[k].wait_recv()
        part = grads_all.at[:, x, :, columns(k)]
        grads_near.append([send(part, part, side) for side in sides])

    for copy in local:
        copy.wait()
    for copy in weights:
        copy.wait_recv()
    for i, distance in enumerate((3, -3)):
        relays[i].wait_recv()
        far[i] = w_back[y_rows(distance, c * HEAD_DIM), :]
        far[i, :, half_columns[i]] = (
            far[i, :, half_columns[i]].astype(F32) + relay[i].astype(F32)
        ).astype(BF16)
        y_moves.append(send(far.at[i], y_in.at[4 + i], y_device(distance)))

    for k in chunks:
        normed_far[k].wait_recv()
        part = normed_part(z, x_at[2], k)
        normed_across[k].append(send(part, part, across))
    grads_far = []
    for k in chunks:
        for i, (side, slot) in enumerate(((right, 3), (left, 1))):
            grads_near[k][i].wait_recv()
            if k % 2 == i:
                part = grads_all.at[:, x_at[slot], :, columns(k)]
                grads_far.append(send(part, part, side))

    acc_back[...] = jnp.zeros_like(acc_back)
    acc_in[...] = jnp.zeros_like(acc_in)
    for k in chunks:
        grads_far[k].wait_recv()
        acc_back[...] += lax.dot_general(
            grads_all[:, :, :, columns(k)].reshape(HALF, GW), w_back[:, columns(k)],
            CONTRACT_LAST, preferred_element_type=F32,
        )
    for k in chunks:
        for copy in normed_across[k]:
            copy.wait_recv()
        acc_in[...] += jnp.dot(
            normed_all[:, :, :, columns(k)].reshape(HALF, GW), w_in[columns(k), :],
            preferred_element_type=F32,
        )

    def blocks(value):
        return value.reshape(8, ROWS, HEAD_DIM)

    first = c == 0

    def column_block(ref, i):
        return ref[:, i * HEAD_DIM : (i + 1) * HEAD_DIM]

    queries = [blocks(column_block(acc_in, i) * width_scale).astype(BF16) for i in range(2)]
    head_grads = [blocks(column_block(acc_back, i) * out_scale).astype(BF16) for i in range(2)]
    keyval = [blocks(column_block(acc_in, i) * width_scale).astype(BF16) for i in (2, 3)]

    def pick(pair, condition):
        return jnp.where(condition, pair[0].astype(F32), pair[1].astype(F32)).astype(BF16)

    heads_out[0] = pick(queries, ~first)
    heads_out[1] = pick(head_grads, ~first)
    heads_out[2] = keyval[0]
    heads_out[3] = keyval[1]
    exchange = send(heads_out, heads.at[:, :, c], sibling)
    heads[0, :, c] = pick(queries, first)
    heads[1, :, c] = pick(head_grads, first)
    heads[2, :, c] = keyval[0]
    heads[3, :, c] = keyval[1]
    exchange.wait_recv()

    def sequence(i):
        return heads[i].astype(F32).reshape(SEQ, HEAD_DIM).astype(BF16)

    query, head_grad, key, value = [sequence(i) for i in range(4)]
    key_parts, value_parts = [None] * 3, [None] * 3
    for i in range(3):
        limit = (i + 1) * 128
        here = slice(i * 128, limit)
        scores = lax.dot_general(
            query[here], key[:limit], CONTRACT_LAST, preferred_element_type=F32
        )
        scores = scores * score_scale + bias[here, :limit]
        powers = jnp.exp(scores - jnp.max(scores, axis=-1, keepdims=True))
        probs = powers / jnp.sum(powers, axis=-1, keepdims=True)
        prob_grads = lax.dot_general(
            head_grad[here], value[:limit], CONTRACT_LAST, preferred_element_type=F32
        )
        score_grads = (
            probs
            * (prob_grads - jnp.sum(probs * prob_grads, axis=-1, keepdims=True))
            * score_scale
        ).astype(BF16)
        probs_low = probs.astype(BF16)
        query_grads = jnp.dot(score_grads, key[:limit], preferred_element_type=F32)
        grad_rows[0, here] = query_grads
        for j in range(i + 1):
            there = slice(j * 128, (j + 1) * 128)
            key_term = lax.dot_general(
                score_grads[:, there], query[here], CONTRACT_FIRST, preferred_element_type=F32
            )
            value_term = lax.dot_general(
                probs_low[:, there], head_grad[here], CONTRACT_FIRST, preferred_element_type=F32
            )
            key_parts[j] = key_term if i == j else key_parts[j] + key_term
            value_parts[j] = value_term if i == j else value_parts[j] + value_term
    for j in range(3):
        there = slice(j * 128, (j + 1) * 128)
        grad_rows[1, there] = key_parts[j]
        grad_rows[2, there] = value_parts[j]
    for i in range(3):
        back[i] = grad_rows[i].reshape(8, 2, ROWS, HEAD_DIM).astype(BF16)
    exchange_back = send(back.at[:, :, other_c], back_in, sibling)

    for copy in y_moves:
        copy.wait_recv()
    total = w_back[y_rows(0, c * HEAD_DIM), :].astype(F32)
    for i in range(6):
        total = total + y_in[i].astype(F32)
    totals[...] = total
    for i in range(Z_HI):
        z_out[i] = totals[i * OUTER_ROWS : (i + 1) * OUTER_ROWS, :].astype(BF16)
    z_moves = []
    for distance in (1, 2, 3):
        owner = lax.rem(zh + distance, Z_HI)
        z_moves.append(send(z_out.at[owner], z_in.at[distance - 1], z_device(distance)))

    exchange_back.wait_recv()

    def own_rows(i):
        return back[i, :, c].astype(F32).reshape(HALF, HEAD_DIM)

    def received_rows(i):
        return back_in[i].astype(F32).reshape(HALF, HEAD_DIM)

    query_pair = (own_rows(0), received_rows(0))
    upstream = jnp.concatenate(
        [
            jnp.where(first, query_pair[0], query_pair[1]).astype(BF16),
            jnp.where(first, query_pair[1], query_pair[0]).astype(BF16),
            (own_rows(1) + received_rows(1)).astype(BF16),
            (own_rows(2) + received_rows(2)).astype(BF16),
        ],
        axis=1,
    )

    def sum_columns(j):
        return pl.ds(j * SW, SW)

    hops, nears, across_moves = {}, {}, {}
    plan = list(enumerate(SUM_PLAN))
    by_x = [(j, way) for j, (kind, way) in plan if kind == "x"]
    by_z = [(j, way) for j, (kind, way) in plan if kind == "z"]
    forward_slot = {0: 1, 1: 3}
    for j, (kind, way) in plan:
        term = lax.dot_general(
            upstream, w_in[sum_columns(j), :], CONTRACT_LAST, preferred_element_type=F32
        )
        terms[:, :, :, sum_columns(j)] = (
            (term * width_scale).reshape(2, 4, ROWS, SW).astype(BF16)
        )
        if kind == "z":
            across_moves[j] = send(
                terms.at[other_z, :, :, sum_columns(j)], from_z_z.at[len(across_moves)], across
            )
        else:
            slot = len(hops)
            forward, backward = forward_slot[way], forward_slot[1 - way]
            hops[j] = send(
                terms.at[:, x_at[2], :, sum_columns(j)], hop_x.at[slot], sides[way]
            )
            nears[j] = [
                send(
                    terms.at[:, x_at[backward], :, sum_columns(j)], near_x.at[slot, 0],
                    sides[1 - way],
                )
            ]

    for slot, (j, way) in enumerate(by_x):
        forward = forward_slot[way]
        hops[j].wait_recv()
        terms[:, x_at[forward], :, sum_columns(j)] = (
            terms[:, x_at[forward], :, sum_columns(j)].astype(F32) + hop_x[slot].astype(F32)
        ).astype(BF16)
        nears[j].append(
            send(
                terms.at[:, x_at[forward], :, sum_columns(j)], near_x.at[slot, 1], sides[way]
            )
        )
    for slot, (j, way) in enumerate(by_z):
        forward, backward = forward_slot[way], forward_slot[1 - way]
        across_moves[j].wait_recv()
        terms[z, :, :, sum_columns(j)] = (
            terms[z, :, :, sum_columns(j)].astype(F32) + from_z_z[slot].astype(F32)
        ).astype(BF16)
        hops[j] = send(terms.at[z, x_at[2], :, sum_columns(j)], hop_z.at[slot], sides[way])
        nears[j] = [
            send(
                terms.at[z, x_at[backward], :, sum_columns(j)], near_z.at[slot, 0],
                sides[1 - way],
            )
        ]
    for slot, (j, way) in enumerate(by_x):
        for copy in nears[j]:
            copy.wait_recv()
        terms[:, x, :, sum_columns(j)] = (
            terms[:, x, :, sum_columns(j)].astype(F32)
            + near_x[slot, 0].astype(F32)
            + near_x[slot, 1].astype(F32)
        ).astype(BF16)
        across_moves[j] = send(
            terms.at[other_z, x, :, sum_columns(j)], from_z_x.at[slot], across
        )
    for slot, (j, way) in enumerate(by_z):
        forward = forward_slot[way]
        hops[j].wait_recv()
        terms[z, x_at[forward], :, sum_columns(j)] = (
            terms[z, x_at[forward], :, sum_columns(j)].astype(F32) + hop_z[slot].astype(F32)
        ).astype(BF16)
        nears[j].append(
            send(
                terms.at[z, x_at[forward], :, sum_columns(j)], near_z.at[slot, 1], sides[way]
            )
        )

    for copy in z_moves:
        copy.wait_recv()
    mean = z_out[zh].astype(F32)
    for i in range(3):
        mean = mean + z_in[i].astype(F32)
    mean = mean * (1.0 / N_REPLICA)
    delta = outer_params[...] - mean
    moment = 0.9 * outer_moment[...] + delta
    new_moment[...] = moment
    new_params[...] = outer_params[...] - 0.7 * (delta + 0.9 * moment)

    normed_grads = [None] * SUMS
    for slot, (j, way) in enumerate(by_x):
        across_moves[j].wait_recv()
        normed_grads[j] = terms[z, x, :, sum_columns(j)].astype(F32) + from_z_x[slot].astype(F32)
    for slot, (j, way) in enumerate(by_z):
        for copy in nears[j]:
            copy.wait_recv()
        normed_grads[j] = (
            terms[z, x, :, sum_columns(j)].astype(F32)
            + near_z[slot, 0].astype(F32)
            + near_z[slot, 1].astype(F32)
        )
    scaled = jnp.concatenate(normed_grads, axis=1) * gain[...]
    centered = inputs[...].astype(F32) * inv_rms
    projected = jnp.sum(scaled * centered, axis=-1, keepdims=True) * (1.0 / D)
    input_grads[...] = (
        out_grads[...].astype(F32) + inv_rms * (scaled - centered * projected)
    ).astype(BF16)
    for copy in sent:
        copy.wait_send()


def on_device(
    inputs, out_grads, norm_gain, doc_ids, w_query, w_keyval, w_out, outer_params, outer_moment
):
    vmem = pl.BlockSpec(memory_space=pltpu.VMEM)
    anywhere = pl.BlockSpec(memory_space=pl.ANY)
    by_x = sum(kind == "x" for kind, _ in SUM_PLAN)
    by_z = SUMS - by_x
    input_grads, new_params, new_moment = pl.pallas_call(
        kernel,
        out_shape=(
            jax.ShapeDtypeStruct((ROWS, D), BF16),
            jax.ShapeDtypeStruct((OUTER_ROWS, D), F32),
            jax.ShapeDtypeStruct((OUTER_ROWS, D), F32),
        ),
        in_specs=[vmem, vmem, vmem, vmem, anywhere, anywhere, anywhere, vmem, vmem],
        out_specs=(vmem, vmem, vmem),
        scratch_shapes=[
            pltpu.VMEM((2, 4, ROWS, D), BF16),
            pltpu.VMEM((2, 4, ROWS, D), BF16),
            pltpu.VMEM((D, 4 * HEAD_DIM), BF16),
            pltpu.VMEM((2 * HEAD_DIM, D), BF16),
            pltpu.VMEM((SEQ, SEQ), F32),
            pltpu.VMEM((HALF, 4 * HEAD_DIM), F32),
            pltpu.VMEM((HALF, 2 * HEAD_DIM), F32),
            pltpu.VMEM((4, 8, 2, ROWS, HEAD_DIM), BF16),
            pltpu.VMEM((4, 8, ROWS, HEAD_DIM), BF16),
            pltpu.VMEM((3, 8, 2, ROWS, HEAD_DIM), BF16),
            pltpu.VMEM((3, 8, ROWS, HEAD_DIM), BF16),
            pltpu.VMEM((3, 8, ROWS, HEAD_DIM), BF16),
            pltpu.VMEM((3, SEQ, HEAD_DIM), F32),
            pltpu.VMEM((2, 4, ROWS, D), BF16),
            pltpu.VMEM((by_x, 2, ROWS, SW), BF16),
            pltpu.VMEM((by_x, 2, 2, ROWS, SW), BF16),
            pltpu.VMEM((by_z, ROWS, SW), BF16),
            pltpu.VMEM((by_z, 2, ROWS, SW), BF16),
            pltpu.VMEM((by_x, ROWS, SW), BF16),
            pltpu.VMEM((by_z, 4, ROWS, SW), BF16),
            pltpu.VMEM((16, D), F32),
            pltpu.VMEM((2, 16, D // 2), BF16),
            pltpu.VMEM((2, 16, D), BF16),
            pltpu.VMEM((6, 16, D), BF16),
            pltpu.VMEM((Z_HI, OUTER_ROWS, D), BF16),
            pltpu.VMEM((Z_HI - 1, OUTER_ROWS, D), BF16),
            pltpu.SemaphoreType.DMA((MAX_SENDS,)),
            pltpu.SemaphoreType.DMA((MAX_SENDS,)),
            pltpu.SemaphoreType.DMA((3,)),
        ],
        compiler_params=pltpu.CompilerParams(
            collective_id=0, has_side_effects=True, vmem_limit_bytes=48 * 2**20
        ),
        name="layer_backward",
    )(
        inputs[0], out_grads[0], norm_gain[None], doc_ids, w_query[0], w_keyval[0], w_out[0],
        outer_params[0], outer_moment[0],
    )
    return input_grads[None], new_params[None], new_moment[None]


def solution(mesh):
    placed = (
        P("replica", "mp", None),
        P("replica", "mp", None),
        P(),
        P("replica", None),
        P("replica", None, "mp"),
        P("replica", None, "mp"),
        P("replica", "mp", None),
        P("mp", "replica", None),
        P("mp", "replica", None),
    )
    return jax.shard_map(
        on_device,
        mesh=mesh,
        in_specs=placed,
        out_specs=(P("replica", "mp", None), P("mp", "replica", None), P("mp", "replica", None)),
        check_vma=False,
    )
```

time: 507 us -> 75.4 us (0.15)
  the two profiles are of different devices: /device:TPU:8 before, /device:TPU:42 now
where the time goes in v1:
time: 75.4 us; the launch traced here: 74.9 us
  Pallas kernels  63.5 us (84%)
  local copies, waits for them, and re-layouts  10.8 us (14%)
    pallas_call x1, Pallas kernels, on_device(): pl.pallas_call(kernel, out_shape=(jax.ShapeDtypeStruct((ROWS, D), BF16),...  63.5 us
    unnamed x19, local copies, waits for them, and re-layouts  10.1 us

profile of v1, /device:TPU:42, one launch (start us, length us, event | category | flops | bytes accessed | tf_op | source)
XLA Modules:
  0.0 74.9 jit_solution(937070877403451217)
XLA Ops:
  0.6 0.7 broadcast_in_dim.12.gain
  1.4 0.0 copy-start
  1.4 1.3 %copy-done = bf16[1,4608,128]{2,1,0:T(8,128)(2,1)S(1)} copy-done((bf16[1,4608,128]{2,1,0:T(8,128)(2,1)S(1)}, bf16[1,4608,128]{2,1,0:T(8,128)(2,1)}, u32[]{:S(2)}) %copy-start) | copy-done | bytes 1179672
  2.6 0.0 copy-start.1
  2.7 1.3 %copy-done.1 = bf16[1,4608,128]{2,1,0:T(8,128)(2,1)S(1)} copy-done((bf16[1,4608,128]{2,1,0:T(8,128)(2,1)S(1)}, bf16[1,4608,128]{2,1,0:T(8,128)(2,1)}, u32[]{:S(2)}) %copy-start.1) | copy-done | bytes 1179672
  3.9 0.0 copy-start.2
  3.9 1.3 %copy-done.2 = bf16[1,128,4608]{2,1,0:T(8,128)(2,1)S(1)} copy-done((bf16[1,128,4608]{2,1,0:T(8,128)(2,1)S(1)}, bf16[1,128,4608]{2,1,0:T(8,128)(2,1)}, u32[]{:S(2)}) %copy-start.2) | copy-done | bytes 1179672
  5.2 0.0 copy-start.3
  5.2 0.9 %copy-done.3 = bf16[1,24,4608]{2,1,0:T(8,128)(2,1)S(1)} copy-done((bf16[1,24,4608]{2,1,0:T(8,128)(2,1)S(1)}, bf16[1,24,4608]{2,1,0:T(8,128)(2,1)}, u32[]{:S(2)}) %copy-start.3) | copy-done | bytes 221208
  6.1 0.0 copy-start.4
  6.1 0.9 %copy-done.4 = bf16[1,24,4608]{2,1,0:T(8,128)(2,1)S(1)} copy-done((bf16[1,24,4608]{2,1,0:T(8,128)(2,1)S(1)}, bf16[1,24,4608]{2,1,0:T(8,128)(2,1)}, u32[]{:S(2)}) %copy-start.4) | copy-done | bytes 221208
  7.1 0.0 copy-start.5
  7.1 0.9 %copy-done.5 = f32[1,4,4608]{2,1,0:T(4,128)S(1)} copy-done((f32[1,4,4608]{2,1,0:T(4,128)S(1)}, f32[1,4,4608]{2,1,0:T(4,128)}, u32[]{:S(2)}) %copy-start.5) | copy-done | bytes 73752
  7.9 0.0 copy-start.6
  8.0 0.9 %copy-done.6 = f32[1,4,4608]{2,1,0:T(4,128)S(1)} copy-done((f32[1,4,4608]{2,1,0:T(4,128)S(1)}, f32[1,4,4608]{2,1,0:T(4,128)}, u32[]{:S(2)}) %copy-start.6) | copy-done | bytes 73752
  8.8 0.0 copy-start.7
  8.8 0.7 copy-done.7
  9.5 63.5 %layer_backward.1 = (bf16[24,4608]{1,0:T(8,128)(2,1)S(1)}, f32[4,4608]{1,0:T(4,128)S(1)}, f32[4,4608]{1,0:T(4,128)S(1)}) custom-call(bf16[24,4608]{1,0:T(8,128)(2,1)S(1)} %bitcast.14, bf16[24,4608]{1,0:T(8,128)(2,1)S(1)} %bitcast.15, f32[1,4608]{1,0:T(1,128)S(1)} %broadcast_in_dim.12.gain, s32[1,384]{1,0:T(1,128)S(1)} %copy-done.7, ...), custom_call_target="tpu_custom_call" | custom-call | tf_op jit(solution)/shard_map/layer_backward/pallas_call | solution.py:424
  73.0 0.7 copy.15
  73.7 0.6 copy.16
  74.3 0.6 copy.17
Async XLA Ops:
  1.4 1.3 %copy-start = (bf16[1,4608,128]{2,1,0:T(8,128)(2,1)S(1)}, bf16[1,4608,128]{2,1,0:T(8,128)(2,1)}, u32[]{:S(2)}) copy-start(bf16[1,4608,128]{2,1,0:T(8,128)(2,1)} %param.13) | copy-start | bytes 3538948
  2.6 1.3 %copy-start.1 = (bf16[1,4608,128]{2,1,0:T(8,128)(2,1)S(1)}, bf16[1,4608,128]{2,1,0:T(8,128)(2,1)}, u32[]{:S(2)}) copy-start(bf16[1,4608,128]{2,1,0:T(8,128)(2,1)} %param.14) | copy-start | bytes 3538948
  3.9 1.3 %copy-start.2 = (bf16[1,128,4608]{2,1,0:T(8,128)(2,1)S(1)}, bf16[1,128,4608]{2,1,0:T(8,128)(2,1)}, u32[]{:S(2)}) copy-start(bf16[1,128,4608]{2,1,0:T(8,128)(2,1)} %param.15) | copy-start | bytes 3538948
  5.2 0.9 %copy-start.3 = (bf16[1,24,4608]{2,1,0:T(8,128)(2,1)S(1)}, bf16[1,24,4608]{2,1,0:T(8,128)(2,1)}, u32[]{:S(2)}) copy-start(bf16[1,24,4608]{2,1,0:T(8,128)(2,1)} %param.9) | copy-start | bytes 663556
  6.1 0.9 %copy-start.4 = (bf16[1,24,4608]{2,1,0:T(8,128)(2,1)S(1)}, bf16[1,24,4608]{2,1,0:T(8,128)(2,1)}, u32[]{:S(2)}) copy-start(bf16[1,24,4608]{2,1,0:T(8,128)(2,1)} %param.10) | copy-start | bytes 663556
  7.1 0.9 %copy-start.5 = (f32[1,4,4608]{2,1,0:T(4,128)S(1)}, f32[1,4,4608]{2,1,0:T(4,128)}, u32[]{:S(2)}) copy-start(f32[1,4,4608]{2,1,0:T(4,128)} %param.16) | copy-start | bytes 221188
  7.9 0.9 %copy-start.6 = (f32[1,4,4608]{2,1,0:T(4,128)S(1)}, f32[1,4,4608]{2,1,0:T(4,128)}, u32[]{:S(2)}) copy-start(f32[1,4,4608]{2,1,0:T(4,128)} %param.17) | copy-start | bytes 221188
  8.8 0.7 copy-start.7

commit v2 on v1

v2 whole, which is shorter than its diff:
```python
import jax
import jax.numpy as jnp
from jax import lax
from jax.experimental import pallas as pl
from jax.experimental.pallas import tpu as pltpu
from jax.sharding import PartitionSpec as P

D = 4608
HEAD_DIM = 128
SEQ = 384
ROWS = 24
HALF = 192
GATHER = 6
GW = D // GATHER
SUMS = 9
SW = D // SUMS
Y_SIZE = 8
Z_HI = 4
OUTER_ROWS = 4
N_REPLICA = 32
MESH = pl.DeviceIdType.MESH
F32 = jnp.float32
BF16 = jnp.bfloat16
CONTRACT_LAST = (((1,), (1,)), ((), ()))
CONTRACT_FIRST = (((0,), (0,)), ((), ()))
N_RECEIVE = 72
N_SEND = 7
N_LOCAL = 8
SUM_PLAN = (
    ("z", 1), ("x", 0), ("z", 1), ("x", 1), ("z", 1), ("x", 0), ("z", 0), ("x", 1), ("x", 0),
)


def kernel(
    inputs_hbm, out_grads_hbm, gain_hbm, docs_hbm, w_query, w_keyval, w_out, params_hbm, moment_hbm,
    input_grads, new_params, new_moment,
    inputs, out_grads, gain, docs, outer_params, outer_moment,
    normed_all, grads_all, w_in, w_back, bias, acc_in, acc_back, heads, heads_out,
    back, back_out, back_in, grad_rows, terms, hop_x, near_x, hop_z, near_z, from_z_x, from_z_z,
    totals, relay, far, y_in, z_out, up_in, up_out, down_in, down_out, mine,
    send_sems, recv_sems, local_sems,
):
    width_scale = D ** (-0.5)
    score_scale = 144.0 ** (-0.5)
    out_scale = (16 * HEAD_DIM) ** (-0.5)
    replica = lax.axis_index("replica")
    model = lax.axis_index("mp")
    c = lax.rem(model, 2)
    x = lax.rem(lax.div(model, 2), 4)
    z = lax.div(model, 8)
    y = lax.div(replica, Z_HI)
    zh = lax.rem(replica, Z_HI)
    other_c = 1 - c
    other_z = 1 - z
    x_at = [lax.rem(x + i, 4) for i in range(4)]

    def on_model(zz, xx, cc):
        return (replica, (zz * 4 + xx) * 2 + cc)

    right = on_model(z, x_at[1], c)
    left = on_model(z, x_at[3], c)
    across = on_model(other_z, x, c)
    sibling = on_model(z, x, other_c)
    sides = (right, left)

    def y_device(distance):
        return (lax.rem(y + distance + Y_SIZE, Y_SIZE) * Z_HI + zh, model)

    def z_device(distance):
        return (replica + distance, model)

    partners = [right, left, across, sibling]
    partners += [y_device(d) for d in (1, -1, 2, -2, 3, -3)]
    barrier = pltpu.get_barrier_semaphore()
    for partner in partners:
        pl.semaphore_signal(barrier, inc=1, device_id=partner, device_id_type=MESH)
    line_steps = ((zh < Z_HI - 1, 1), (zh > 0, -1))
    for has_neighbour, step in line_steps:

        @pl.when(has_neighbour)
        def _():
            pl.semaphore_signal(
                barrier, inc=1, device_id=z_device(step), device_id_type=MESH
            )

    own_columns = pl.ds(pl.multiple_of(c * HEAD_DIM, HEAD_DIM), HEAD_DIM)
    own_keyval = pl.ds(pl.multiple_of(2 * HEAD_DIM + c * HEAD_DIM, HEAD_DIM), HEAD_DIM)
    weight_moves = (
        (w_out, w_back.at[own_columns, :]),
        (w_query, w_in.at[:, own_columns]),
        (w_keyval, w_in.at[:, own_keyval]),
    )
    moves = (
        (inputs_hbm, inputs),
        (gain_hbm, gain.at[0]),
        (out_grads_hbm, grads_all.at[z, x]),
        (docs_hbm, docs),
        (out_grads_hbm, out_grads),
        (params_hbm, outer_params),
        (moment_hbm, outer_moment),
    ) + weight_moves
    local = []
    for index, (src, dst) in enumerate(moves):
        copy = pltpu.make_async_copy(src, dst, local_sems.at[min(index, N_LOCAL - 1)])
        copy.start()
        local.append(copy)

    receivers = iter(range(N_RECEIVE))

    def receiver():
        return recv_sems.at[next(receivers)]

    def send(src, dst, device, arrival, group=0):
        copy = pltpu.make_async_remote_copy(
            src_ref=src, dst_ref=dst, send_sem=send_sems.at[group], recv_sem=arrival,
            device_id=device, device_id_type=MESH,
        )
        copy.start()

    def wait_bytes_of(ref, semaphore):
        pltpu.make_async_copy(ref, ref, semaphore).wait()

    local[0].wait()
    rows = inputs[...].astype(F32)
    inv_rms = lax.rsqrt(jnp.sum(rows * rows, axis=-1, keepdims=True) * (1.0 / D) + 1e-06)
    local[1].wait()
    normed_all[z, x] = (rows * inv_rms * gain[...]).astype(BF16)
    local[2].wait()

    line_neighbours = 1 + lax.rem(lax.div(zh + 1, 2), 2)
    pl.semaphore_wait(barrier, len(partners) + line_neighbours)

    def columns(k):
        return pl.ds(k * GW, GW)

    def normed_part(zz, xx, k):
        return normed_all.at[zz, xx, :, columns(k)]

    def grads_part(zz, xx, k):
        return grads_all.at[zz, xx, :, columns(k)]

    chunks = range(GATHER)
    z_first = GATHER - 1
    grads_crossed, grads_near, grads_far = [[receiver() for _ in chunks] for _ in range(3)]
    normed_near, normed_far, normed_crossed = [[receiver() for _ in chunks] for _ in range(3)]
    for k in chunks:
        part = grads_part(z, x, k)
        send(part, part, across, grads_crossed[k])
        part = normed_part(z, x, k)
        for side in sides:
            send(part, part, side, normed_near[k])
    for k in chunks:
        part = normed_part(z, x, k)
        send(part, part, across, normed_crossed[k])

    def y_rows(distance, base=0):
        owner = lax.rem(y + distance + Y_SIZE, Y_SIZE)
        return pl.ds(pl.multiple_of(base + owner * 16, 16), 16)

    half_columns = (pl.ds(0, D // 2), pl.ds(D // 2, D // 2))
    relayed, weighed, summed = receiver(), receiver(), receiver()
    for i, distance in enumerate((1, -1)):
        send(w_out.at[y_rows(4), half_columns[i]], relay.at[i], y_device(distance), relayed)
    for src, dst in weight_moves:
        send(src, dst, sibling, weighed, 1)
    for i, distance in enumerate((1, -1, 2, -2)):
        send(w_out.at[y_rows(distance), :], y_in.at[i], y_device(distance), summed)

    local[3].wait()
    row_at = lax.broadcasted_iota(jnp.int32, (SEQ, SEQ), 0)
    column_at = lax.broadcasted_iota(jnp.int32, (SEQ, SEQ), 1)
    documents = jnp.broadcast_to(docs[...].astype(F32), (SEQ, SEQ))
    own_document = jnp.sum(
        jnp.where(row_at == column_at, documents, 0.0), axis=-1, keepdims=True
    )
    allowed = (column_at <= row_at) & (documents == own_document)
    bias[...] = jnp.where(allowed, 0.0, -1e30)

    def from_side(i):
        return (3, 1)[i]

    for k in chunks:
        wait_bytes_of(normed_all.at[z, pl.ds(0, 2), :, columns(k)], normed_near[k])
        part = normed_part(z, x_at[from_side(k % 2)], k)
        send(part, part, sides[k % 2], normed_far[k])
        if k != z_first:
            for i in range(2):
                part = normed_part(z, x_at[from_side(i)], k)
                send(part, part, across, normed_crossed[k])
        wait_bytes_of(grads_part(other_z, x, k), grads_crossed[k])
        part = grads_all.at[:, x, :, columns(k)]
        for side in sides:
            send(part, part, side, grads_near[k])

    for copy in local[4 : N_LOCAL - 1]:
        copy.wait()
    all_weights = w_in.at[pl.ds(0, 3456), :]
    wait_bytes_of(all_weights, local_sems.at[N_LOCAL - 1])
    wait_bytes_of(all_weights, weighed)
    wait_bytes_of(relay, relayed)
    for i, distance in enumerate((3, -3)):
        far[i] = w_back[y_rows(distance, c * HEAD_DIM), :]
        far[i, :, half_columns[i]] = (
            far[i, :, half_columns[i]].astype(F32) + relay[i].astype(F32)
        ).astype(BF16)
        send(far.at[i], y_in.at[4 + i], y_device(distance), summed)

    wait_bytes_of(normed_part(other_z, x, z_first), normed_crossed[z_first])
    part = normed_part(other_z, x, z_first)
    crossed_near, crossed_far = receiver(), receiver()
    for side in sides:
        send(part, part, side, crossed_near)
    for k in chunks:
        wait_bytes_of(normed_part(z, x_at[2], k), normed_far[k])
        if k != z_first:
            part = normed_part(z, x_at[2], k)
            send(part, part, across, normed_crossed[k])
    for k in chunks:
        wait_bytes_of(grads_all.at[:, pl.ds(0, 2), :, columns(k)], grads_near[k])
        part = grads_all.at[:, x_at[from_side(k % 2)], :, columns(k)]
        send(part, part, sides[k % 2], grads_far[k])
        if k == 1:
            wait_bytes_of(normed_all.at[z, pl.ds(0, 2), :, columns(z_first)], crossed_near)
            part = normed_part(other_z, x_at[from_side(z_first % 2)], z_first)
            send(part, part, sides[z_first % 2], crossed_far)

    acc_back[...] = jnp.zeros_like(acc_back)
    acc_in[...] = jnp.zeros_like(acc_in)
    for k in chunks:
        wait_bytes_of(grads_all.at[:, x_at[2], :, columns(k)], grads_far[k])
        acc_back[...] += lax.dot_general(
            grads_all[:, :, :, columns(k)].reshape(HALF, GW), w_back[:, columns(k)],
            CONTRACT_LAST, preferred_element_type=F32,
        )
    wait_bytes_of(y_in, summed)
    total = w_back[y_rows(0, c * HEAD_DIM), :].astype(F32)
    for i in range(6):
        total = total + y_in[i].astype(F32)
    totals[...] = total
    for i in range(Z_HI):
        z_out[i] = totals[i * OUTER_ROWS : (i + 1) * OUTER_ROWS, :].astype(BF16)
    line = {}

    upward, downward = receiver(), receiver()

    def line_copy(name, src, dst, step):
        line[name] = pltpu.make_async_remote_copy(
            src_ref=src, dst_ref=dst, send_sem=send_sems.at[2 if step > 0 else 3],
            recv_sem=upward if step > 0 else downward,
            device_id=z_device(step), device_id_type=MESH,
        )

    line_copy("up0", z_out.at[pl.ds(1, 3)], up_in, 1)
    line_copy("up1", up_out.at[pl.ds(0, 2)], up_in.at[pl.ds(1, 2)], 1)
    line_copy("up2", up_out.at[pl.ds(2, 1)], up_in.at[pl.ds(2, 1)], 1)
    line_copy("down3", z_out.at[pl.ds(0, 3)], down_in, -1)
    line_copy("down2", down_out.at[pl.ds(0, 2)], down_in.at[pl.ds(0, 2)], -1)
    line_copy("down1", down_out.at[pl.ds(2, 1)], down_in.at[pl.ds(0, 1)], -1)

    def at(position):
        return pl.when(zh == position)

    def line_sum(first, second):
        return (first.astype(F32) + second.astype(F32)).astype(BF16)

    @at(0)
    def _():
        line["up0"].start()

    @at(3)
    def _():
        line["down3"].start()

    for k in chunks:
        if k == z_first:
            wait_bytes_of(normed_part(other_z, x_at[2], k), crossed_far)
        else:
            wait_bytes_of(normed_all.at[other_z, :, :, columns(k)], normed_crossed[k])
        acc_in[...] += jnp.dot(
            normed_all[:, :, :, columns(k)].reshape(HALF, GW), w_in[columns(k), :],
            preferred_element_type=F32,
        )

    def blocks(value):
        return value.reshape(8, ROWS, HEAD_DIM)

    first = c == 0

    def column_block(ref, i):
        return ref[:, i * HEAD_DIM : (i + 1) * HEAD_DIM]

    queries = [blocks(column_block(acc_in, i) * width_scale).astype(BF16) for i in range(2)]
    head_grads = [blocks(column_block(acc_back, i) * out_scale).astype(BF16) for i in range(2)]
    keyval = [blocks(column_block(acc_in, i) * width_scale).astype(BF16) for i in (2, 3)]

    def pick(pair, condition):
        return jnp.where(condition, pair[0].astype(F32), pair[1].astype(F32)).astype(BF16)

    heads_out[0] = pick(queries, ~first)
    heads_out[1] = pick(head_grads, ~first)
    heads_out[2] = keyval[0]
    heads_out[3] = keyval[1]
    exchanged, returned = receiver(), receiver()
    send(heads_out, heads.at[:, :, c], sibling, exchanged)
    heads[0, :, c] = pick(queries, first)
    heads[1, :, c] = pick(head_grads, first)
    heads[2, :, c] = keyval[0]
    heads[3, :, c] = keyval[1]
    wait_bytes_of(heads_out, exchanged)

    def sequence(i):
        return heads[i].astype(F32).reshape(SEQ, HEAD_DIM).astype(BF16)

    query, head_grad, key, value = [sequence(i) for i in range(4)]
    key_parts, value_parts = [None] * 3, [None] * 3
    for i in range(3):
        limit = (i + 1) * 128
        here = slice(i * 128, limit)
        scores = lax.dot_general(
            query[here], key[:limit], CONTRACT_LAST, preferred_element_type=F32
        )
        scores = scores * score_scale + bias[here, :limit]
        powers = jnp.exp(scores - jnp.max(scores, axis=-1, keepdims=True))
        probs = powers / jnp.sum(powers, axis=-1, keepdims=True)
        prob_grads = lax.dot_general(
            head_grad[here], value[:limit], CONTRACT_LAST, preferred_element_type=F32
        )
        score_grads = (
            probs
            * (prob_grads - jnp.sum(probs * prob_grads, axis=-1, keepdims=True))
            * score_scale
        ).astype(BF16)
        probs_low = probs.astype(BF16)
        query_grads = jnp.dot(score_grads, key[:limit], preferred_element_type=F32)
        grad_rows[0, here] = query_grads
        for j in range(i + 1):
            there = slice(j * 128, (j + 1) * 128)
            key_term = lax.dot_general(
                score_grads[:, there], query[here], CONTRACT_FIRST, preferred_element_type=F32
            )
            value_term = lax.dot_general(
                probs_low[:, there], head_grad[here], CONTRACT_FIRST, preferred_element_type=F32
            )
            key_parts[j] = key_term if i == j else key_parts[j] + key_term
            value_parts[j] = value_term if i == j else value_parts[j] + value_term
    for j in range(3):
        there = slice(j * 128, (j + 1) * 128)
        grad_rows[1, there] = key_parts[j]
        grad_rows[2, there] = value_parts[j]
    for i in range(3):
        back[i] = grad_rows[i].reshape(8, 2, ROWS, HEAD_DIM).astype(BF16)
    send(back.at[:, :, other_c], back_in, sibling, returned)

    @at(1)
    def _():
        line["up0"].wait_recv()
        up_out[0:2] = line_sum(z_out[2:4], up_in[1:3])
        line["up1"].start()

    @at(2)
    def _():
        line["down3"].wait_recv()
        down_out[0:2] = line_sum(z_out[0:2], down_in[0:2])
        line["down2"].start()

    wait_bytes_of(back_in, returned)

    def own_rows(i):
        return back[i, :, c].astype(F32).reshape(HALF, HEAD_DIM)

    def received_rows(i):
        return back_in[i].astype(F32).reshape(HALF, HEAD_DIM)

    query_pair = (own_rows(0), received_rows(0))
    upstream = jnp.concatenate(
        [
            jnp.where(first, query_pair[0], query_pair[1]).astype(BF16),
            jnp.where(first, query_pair[1], query_pair[0]).astype(BF16),
            (own_rows(1) + received_rows(1)).astype(BF16),
            (own_rows(2) + received_rows(2)).astype(BF16),
        ],
        axis=1,
    )

    def sum_columns(j):
        return pl.ds(j * SW, SW)

    hopped, neared, crossed = [[receiver() for _ in range(SUMS)] for _ in range(3)]
    plan = list(enumerate(SUM_PLAN))
    by_x = [(j, way) for j, (kind, way) in plan if kind == "x"]
    by_z = [(j, way) for j, (kind, way) in plan if kind == "z"]
    slot_of = {j: slot for group in (by_x, by_z) for slot, (j, _) in enumerate(group)}
    forward_slot = {0: 1, 1: 3}
    for j, (kind, way) in plan:
        term = lax.dot_general(
            upstream, w_in[sum_columns(j), :], CONTRACT_LAST, preferred_element_type=F32
        )
        terms[:, :, :, sum_columns(j)] = (
            (term * width_scale).reshape(2, 4, ROWS, SW).astype(BF16)
        )
        slot = slot_of[j]
        if kind == "z":
            part = terms.at[other_z, :, :, sum_columns(j)]
            send(part, from_z_z.at[slot], across, crossed[j], 4)
        else:
            part = terms.at[:, x_at[2], :, sum_columns(j)]
            send(part, hop_x.at[slot], sides[way], hopped[j], 5)
            part = terms.at[:, x_at[forward_slot[1 - way]], :, sum_columns(j)]
            send(part, near_x.at[slot, 0], sides[1 - way], neared[j], 5)

    for slot, (j, way) in enumerate(by_x):
        forward = forward_slot[way]
        wait_bytes_of(hop_x.at[slot], hopped[j])
        terms[:, x_at[forward], :, sum_columns(j)] = (
            terms[:, x_at[forward], :, sum_columns(j)].astype(F32) + hop_x[slot].astype(F32)
        ).astype(BF16)
        part = terms.at[:, x_at[forward], :, sum_columns(j)]
        send(part, near_x.at[slot, 1], sides[way], neared[j], 5)
    for slot, (j, way) in enumerate(by_z):
        wait_bytes_of(from_z_z.at[slot], crossed[j])
        terms[z, :, :, sum_columns(j)] = (
            terms[z, :, :, sum_columns(j)].astype(F32) + from_z_z[slot].astype(F32)
        ).astype(BF16)
        part = terms.at[z, x_at[2], :, sum_columns(j)]
        send(part, hop_z.at[slot], sides[way], hopped[j], 4)
        part = terms.at[z, x_at[forward_slot[1 - way]], :, sum_columns(j)]
        send(part, near_z.at[slot, 0], sides[1 - way], neared[j], 4)

    @at(2)
    def _():
        line["up1"].wait_recv()
        up_out[2:3] = line_sum(z_out[3:4], up_in[2:3])
        line["up2"].start()

    @at(1)
    def _():
        line["down2"].wait_recv()
        down_out[2:3] = line_sum(z_out[0:1], down_in[0:1])
        line["down1"].start()

    for slot, (j, way) in enumerate(by_x):
        wait_bytes_of(near_x.at[slot], neared[j])
        terms[:, x, :, sum_columns(j)] = (
            terms[:, x, :, sum_columns(j)].astype(F32)
            + near_x[slot, 0].astype(F32)
            + near_x[slot, 1].astype(F32)
        ).astype(BF16)
        part = terms.at[other_z, x, :, sum_columns(j)]
        send(part, from_z_x.at[slot], across, crossed[j], 6)
    for slot, (j, way) in enumerate(by_z):
        forward = forward_slot[way]
        wait_bytes_of(hop_z.at[slot], hopped[j])
        terms[z, x_at[forward], :, sum_columns(j)] = (
            terms[z, x_at[forward], :, sum_columns(j)].astype(F32) + hop_z[slot].astype(F32)
        ).astype(BF16)
        part = terms.at[z, x_at[forward], :, sum_columns(j)]
        send(part, near_z.at[slot, 1], sides[way], neared[j], 4)

    @at(0)
    def _():
        line["down1"].wait_recv()
        mine[...] = z_out[0].astype(F32) + down_in[0].astype(F32)

    @at(1)
    def _():
        mine[...] = z_out[1].astype(F32) + up_in[0].astype(F32) + down_in[1].astype(F32)

    @at(2)
    def _():
        mine[...] = z_out[2].astype(F32) + up_in[1].astype(F32) + down_in[2].astype(F32)

    @at(3)
    def _():
        line["up2"].wait_recv()
        mine[...] = z_out[3].astype(F32) + up_in[2].astype(F32)

    mean = mine[...]
    mean = mean * (1.0 / N_REPLICA)
    delta = outer_params[...] - mean
    moment = 0.9 * outer_moment[...] + delta
    new_moment[...] = moment
    new_params[...] = outer_params[...] - 0.7 * (delta + 0.9 * moment)

    normed_grads = [None] * SUMS
    for slot, (j, way) in enumerate(by_x):
        wait_bytes_of(from_z_x.at[slot], crossed[j])
        normed_grads[j] = terms[z, x, :, sum_columns(j)].astype(F32) + from_z_x[slot].astype(F32)
    for slot, (j, way) in enumerate(by_z):
        wait_bytes_of(near_z.at[slot], neared[j])
        normed_grads[j] = (
            terms[z, x, :, sum_columns(j)].astype(F32)
            + near_z[slot, 0].astype(F32)
            + near_z[slot, 1].astype(F32)
        )
    scaled = jnp.concatenate(normed_grads, axis=1) * gain[...]
    centered = inputs[...].astype(F32) * inv_rms
    projected = jnp.sum(scaled * centered, axis=-1, keepdims=True) * (1.0 / D)
    input_grads[...] = (
        out_grads[...].astype(F32) + inv_rms * (scaled - centered * projected)
    ).astype(BF16)
    assert next(receivers, None) is None
    wait_bytes_of(w_in.at[pl.ds(0, 4368), :], send_sems.at[0])
    wait_bytes_of(all_weights, send_sems.at[1])
    wait_bytes_of(terms.at[0, :, :, pl.ds(0, 7 * SW)], send_sems.at[4])
    wait_bytes_of(terms.at[:, pl.ds(0, 3), :, pl.ds(0, 5 * SW)], send_sems.at[5])
    wait_bytes_of(terms.at[0, 0, :, pl.ds(0, 5 * SW)], send_sems.at[6])
    for position, names in enumerate((("up0",), ("up1", "down1"), ("up2", "down2"), ("down3",))):

        @at(position)
        def _():
            for name in names:
                line[name].wait_send()


def write_out(first, second, third, first_out, second_out, third_out, *scratch):
    held, (in_sems, out_sems) = scratch[:3], scratch[3:]
    results = (first_out, second_out, third_out)
    loads = [
        pltpu.make_async_copy(src, held[i], in_sems.at[i])
        for i, src in enumerate((first, second, third))
    ]
    stores = [
        pltpu.make_async_copy(held[i], dst.at[0], out_sems.at[i]) for i, dst in enumerate(results)
    ]
    for load in loads:
        load.start()
    for load, store in zip(loads, stores):
        load.wait()
        store.start()
    for store in stores:
        store.wait()


def on_device(
    inputs, out_grads, norm_gain, doc_ids, w_query, w_keyval, w_out, outer_params, outer_moment
):
    vmem = pl.BlockSpec(memory_space=pltpu.VMEM)
    hbm = pl.BlockSpec(memory_space=pltpu.HBM)
    anywhere = pl.BlockSpec(memory_space=pl.ANY)
    by_x = sum(kind == "x" for kind, _ in SUM_PLAN)
    by_z = SUMS - by_x
    input_grads, new_params, new_moment = pl.pallas_call(
        kernel,
        out_shape=(
            jax.ShapeDtypeStruct((ROWS, D), BF16),
            jax.ShapeDtypeStruct((OUTER_ROWS, D), F32),
            jax.ShapeDtypeStruct((OUTER_ROWS, D), F32),
        ),
        in_specs=[hbm] * 9,
        out_specs=(vmem, vmem, vmem),
        scratch_shapes=[
            pltpu.VMEM((ROWS, D), BF16),
            pltpu.VMEM((ROWS, D), BF16),
            pltpu.VMEM((1, D), F32),
            pltpu.VMEM((1, SEQ), jnp.int32),
            pltpu.VMEM((OUTER_ROWS, D), F32),
            pltpu.VMEM((OUTER_ROWS, D), F32),
            pltpu.VMEM((2, 4, ROWS, D), BF16),
            pltpu.VMEM((2, 4, ROWS, D), BF16),
            pltpu.VMEM((D, 4 * HEAD_DIM), BF16),
            pltpu.VMEM((2 * HEAD_DIM, D), BF16),
            pltpu.VMEM((SEQ, SEQ), F32),
            pltpu.VMEM((HALF, 4 * HEAD_DIM), F32),
            pltpu.VMEM((HALF, 2 * HEAD_DIM), F32),
            pltpu.VMEM((4, 8, 2, ROWS, HEAD_DIM), BF16),
            pltpu.VMEM((4, 8, ROWS, HEAD_DIM), BF16),
            pltpu.VMEM((3, 8, 2, ROWS, HEAD_DIM), BF16),
            pltpu.VMEM((3, 8, ROWS, HEAD_DIM), BF16),
            pltpu.VMEM((3, 8, ROWS, HEAD_DIM), BF16),
            pltpu.VMEM((3, SEQ, HEAD_DIM), F32),
            pltpu.VMEM((2, 4, ROWS, D), BF16),
            pltpu.VMEM((by_x, 2, ROWS, SW), BF16),
            pltpu.VMEM((by_x, 2, 2, ROWS, SW), BF16),
            pltpu.VMEM((by_z, ROWS, SW), BF16),
            pltpu.VMEM((by_z, 2, ROWS, SW), BF16),
            pltpu.VMEM((by_x, ROWS, SW), BF16),
            pltpu.VMEM((by_z, 4, ROWS, SW), BF16),
            pltpu.VMEM((16, D), F32),
            pltpu.VMEM((2, 16, D // 2), BF16),
            pltpu.VMEM((2, 16, D), BF16),
            pltpu.VMEM((6, 16, D), BF16),
            pltpu.VMEM((Z_HI, OUTER_ROWS, D), BF16),
            pltpu.VMEM((Z_HI - 1, OUTER_ROWS, D), BF16),
            pltpu.VMEM((Z_HI - 1, OUTER_ROWS, D), BF16),
            pltpu.VMEM((Z_HI - 1, OUTER_ROWS, D), BF16),
            pltpu.VMEM((Z_HI - 1, OUTER_ROWS, D), BF16),
            pltpu.VMEM((OUTER_ROWS, D), F32),
            pltpu.SemaphoreType.DMA((N_SEND,)),
            pltpu.SemaphoreType.DMA((N_RECEIVE,)),
            pltpu.SemaphoreType.DMA((N_LOCAL,)),
        ],
        compiler_params=pltpu.CompilerParams(
            collective_id=0, has_side_effects=True, vmem_limit_bytes=63 * 2**20
        ),
        name="layer_backward",
    )(
        inputs[0], out_grads[0], norm_gain, doc_ids, w_query[0], w_keyval[0], w_out[0],
        outer_params[0], outer_moment[0],
    )
    input_grads, new_params, new_moment = pl.pallas_call(
        write_out,
        out_shape=(
            jax.ShapeDtypeStruct((1, ROWS, D), BF16),
            jax.ShapeDtypeStruct((1, OUTER_ROWS, D), F32),
            jax.ShapeDtypeStruct((1, OUTER_ROWS, D), F32),
        ),
        in_specs=[anywhere] * 3,
        out_specs=[anywhere] * 3,
        scratch_shapes=[
            pltpu.VMEM((ROWS, D), BF16),
            pltpu.VMEM((OUTER_ROWS, D), F32),
            pltpu.VMEM((OUTER_ROWS, D), F32),
            pltpu.SemaphoreType.DMA((3,)),
            pltpu.SemaphoreType.DMA((3,)),
        ],
        compiler_params=pltpu.CompilerParams(vmem_limit_bytes=63 * 2**20),
        name="write_out",
    )(input_grads, new_params, new_moment)
    return input_grads, new_params, new_moment


def solution(mesh):
    placed = (
        P("replica", "mp", None),
        P("replica", "mp", None),
        P(),
        P("replica", None),
        P("replica", None, "mp"),
        P("replica", None, "mp"),
        P("replica", "mp", None),
        P("mp", "replica", None),
        P("mp", "replica", None),
    )
    return jax.shard_map(
        on_device,
        mesh=mesh,
        in_specs=placed,
        out_specs=(P("replica", "mp", None), P("mp", "replica", None), P("mp", "replica", None)),
        check_vma=False,
    )
```

time: 75.4 us -> 62.7 us (0.83)
  the two profiles are of different devices: /device:TPU:42 before, /device:TPU:130 now
where the time goes in v2:
time: 62.7 us; the launch traced here: 62.5 us
  Pallas kernels  61.9 us (99%)
  between operations  0.64 us (1%)
    pallas_call x1, Pallas kernels, on_device(): pl.pallas_call(kernel, out_shape=(jax.ShapeDtypeStruct((ROWS, D), BF16),...  60.2 us
    pallas_call x1, Pallas kernels, on_device(): pl.pallas_call(write_out, out_shape=(jax.ShapeDtypeStruct((1, ROWS, D), B...  1.72 us

profile of v2, /device:TPU:130, one launch (start us, length us, event | category | flops | bytes accessed | tf_op | source)
XLA Modules:
  0.0 62.5 jit_solution(3831801113996862075)
XLA Ops:
  0.6 60.2 %layer_backward.1 = (bf16[24,4608]{1,0:T(8,128)(2,1)}, f32[4,4608]{1,0:T(4,128)}, f32[4,4608]{1,0:T(4,128)}) custom-call(bf16[24,4608]{1,0:T(8,128)(2,1)} %bitcast.10, bf16[24,4608]{1,0:T(8,128)(2,1)} %bitcast.11, f32[4608]{0:T(1024)} %gain_hbm.1, s32[1,384]{1,0:T(1,128)} %docs_hbm.1, bf16[4608,128]{1,0:T(8,128)(2,1)} %bitcast.7, bf16[4608,128]{1,0:T(8,128)(2,1)} %bitcast.8, ...), custom_call_target="tpu_custom_call" | custom-call | tf_op jit(solution)/shard_map/layer_backward/pallas_call | solution.py:542
  60.8 1.7 %write_out.1 = (bf16[1,24,4608]{2,1,0:T(8,128)(2,1)}, f32[1,4,4608]{2,1,0:T(4,128)}, f32[1,4,4608]{2,1,0:T(4,128)}) custom-call(bf16[24,4608]{1,0:T(8,128)(2,1)} %get-tuple-element.6.first, f32[4,4608]{1,0:T(4,128)} %get-tuple-element.7.second, f32[4,4608]{1,0:T(4,128)} %get-tuple-element.8.third), custom_call_target="tpu_custom_call" | custom-call | tf_op jit(solution)/shard_map/write_out/pallas_call | solution.py:600

commit v3 on v2

--- a/solution.py
+++ b/solution.py
@@ -12,7 +12,7 @@
 HALF = 192
 GATHER = 6
 GW = D // GATHER
-SUMS = 9
+SUMS = 12
 SW = D // SUMS
 Y_SIZE = 8
 Z_HI = 4
@@ -23,11 +23,11 @@
 BF16 = jnp.bfloat16
 CONTRACT_LAST = (((1,), (1,)), ((), ()))
 CONTRACT_FIRST = (((0,), (0,)), ((), ()))
-N_RECEIVE = 72
-N_SEND = 7
+N_RECEIVE = 82
+N_SEND = 8
 N_LOCAL = 8
 SUM_PLAN = (
-    ("z", 1), ("x", 0), ("z", 1), ("x", 1), ("z", 1), ("x", 0), ("z", 0), ("x", 1), ("x", 0),
+    ("z", 1), ("x", 0), ("z", 0), ("x", 1), ("z", 1), ("x", 0), ("x", 1), ("z", 0), ("x", 0), ("x", 1), ("x", 0), ("x", 1),
 )
 
 
@@ -38,7 +38,7 @@
     normed_all, grads_all, w_in, w_back, bias, acc_in, acc_back, heads, heads_out,
     back, back_out, back_in, grad_rows, terms, hop_x, near_x, hop_z, near_z, from_z_x, from_z_z,
     totals, relay, far, y_in, z_out, up_in, up_out, down_in, down_out, mine,
-    send_sems, recv_sems, local_sems,
+    send_sems, recv_sems, local_sems, meet,
 ):
     width_scale = D ** (-0.5)
     score_scale = 144.0 ** (-0.5)
@@ -70,18 +70,21 @@
         return (replica + distance, model)
 
     partners = [right, left, across, sibling]
-    partners += [y_device(d) for d in (1, -1, 2, -2, 3, -3)]
+    partners += [y_device(d) for d in (1, -1)]
+    outward = 2 * z - 1
+    has_outward = jnp.where(z == 1, zh < Z_HI - 1, zh > 0)
+    outward_device = (replica + outward, (other_z * 4 + x) * 2 + c)
+
+    def signal(semaphore, device):
+        pl.semaphore_signal(semaphore, inc=1, device_id=device, device_id_type=MESH)
+
     barrier = pltpu.get_barrier_semaphore()
     for partner in partners:
-        pl.semaphore_signal(barrier, inc=1, device_id=partner, device_id_type=MESH)
-    line_steps = ((zh < Z_HI - 1, 1), (zh > 0, -1))
-    for has_neighbour, step in line_steps:
-
-        @pl.when(has_neighbour)
-        def _():
-            pl.semaphore_signal(
-                barrier, inc=1, device_id=z_device(step), device_id_type=MESH
-            )
+        signal(barrier, partner)
+
+    @pl.when(has_outward)
+    def _():
+        signal(barrier, outward_device)
 
     own_columns = pl.ds(pl.multiple_of(c * HEAD_DIM, HEAD_DIM), HEAD_DIM)
     own_keyval = pl.ds(pl.multiple_of(2 * HEAD_DIM + c * HEAD_DIM, HEAD_DIM), HEAD_DIM)
@@ -127,8 +130,13 @@
     normed_all[z, x] = (rows * inv_rms * gain[...]).astype(BF16)
     local[2].wait()
 
-    line_neighbours = 1 + lax.rem(lax.div(zh + 1, 2), 2)
-    pl.semaphore_wait(barrier, len(partners) + line_neighbours)
+    @pl.when(has_outward)
+    def _():
+        pl.semaphore_wait(barrier, len(partners) + 1)
+
+    @pl.when(~has_outward)
+    def _():
+        pl.semaphore_wait(barrier, len(partners))
 
     def columns(k):
         return pl.ds(k * GW, GW)
@@ -141,17 +149,32 @@
 
     chunks = range(GATHER)
     z_first = GATHER - 1
-    grads_crossed, grads_near, grads_far = [[receiver() for _ in chunks] for _ in range(3)]
-    normed_near, normed_far, normed_crossed = [[receiver() for _ in chunks] for _ in range(3)]
+    normed_crossed, normed_near, normed_far = [[receiver() for _ in chunks] for _ in range(3)]
+    grads_near, grads_far, grads_crossed = [[receiver() for _ in chunks] for _ in range(3)]
+    for k in chunks:
+        part = normed_part(z, x, k)
+        send(part, part, across, normed_crossed[k])
+        part = grads_part(z, x, k)
+        for side in sides:
+            send(part, part, side, grads_near[k])
     for k in chunks:
         part = grads_part(z, x, k)
         send(part, part, across, grads_crossed[k])
-        part = normed_part(z, x, k)
-        for side in sides:
-            send(part, part, side, normed_near[k])
-    for k in chunks:
-        part = normed_part(z, x, k)
-        send(part, part, across, normed_crossed[k])
+
+    y_far = {2: meet.at[0], -2: meet.at[1], 3: meet.at[2], -3: meet.at[3]}
+    line_up, line_down = meet.at[4], meet.at[5]
+    signal(y_far[2], y_device(-1))
+    signal(y_far[-2], y_device(1))
+
+    @pl.when((z == 1) & has_outward)
+    def _():
+        signal(line_up, across)
+        signal(line_down, outward_device)
+
+    @pl.when((z == 0) & has_outward)
+    def _():
+        signal(line_down, across)
+        signal(line_up, outward_device)
 
     def y_rows(distance, base=0):
         owner = lax.rem(y + distance + Y_SIZE, Y_SIZE)
@@ -163,7 +186,7 @@
         send(w_out.at[y_rows(4), half_columns[i]], relay.at[i], y_device(distance), relayed)
     for src, dst in weight_moves:
         send(src, dst, sibling, weighed, 1)
-    for i, distance in enumerate((1, -1, 2, -2)):
+    for i, distance in enumerate((1, -1)):
         send(w_out.at[y_rows(distance), :], y_in.at[i], y_device(distance), summed)
 
     local[3].wait()
@@ -176,21 +199,27 @@
     allowed = (column_at <= row_at) & (documents == own_document)
     bias[...] = jnp.where(allowed, 0.0, -1e30)
 
+    for i, distance in enumerate((2, -2)):
+        pl.semaphore_wait(y_far[distance], 1)
+        send(w_out.at[y_rows(distance), :], y_in.at[2 + i], y_device(distance), summed)
+    signal(y_far[3], y_device(-1))
+    signal(y_far[-3], y_device(2))
+
     def from_side(i):
         return (3, 1)[i]
 
     for k in chunks:
-        wait_bytes_of(normed_all.at[z, pl.ds(0, 2), :, columns(k)], normed_near[k])
-        part = normed_part(z, x_at[from_side(k % 2)], k)
-        send(part, part, sides[k % 2], normed_far[k])
+        wait_bytes_of(grads_all.at[z, pl.ds(0, 2), :, columns(k)], grads_near[k])
+        part = grads_part(z, x_at[from_side(k % 2)], k)
+        send(part, part, sides[k % 2], grads_far[k])
         if k != z_first:
             for i in range(2):
-                part = normed_part(z, x_at[from_side(i)], k)
-                send(part, part, across, normed_crossed[k])
-        wait_bytes_of(grads_part(other_z, x, k), grads_crossed[k])
-        part = grads_all.at[:, x, :, columns(k)]
+                part = grads_part(z, x_at[from_side(i)], k)
+                send(part, part, across, grads_crossed[k])
+        wait_bytes_of(normed_part(other_z, x, k), normed_crossed[k])
+        part = normed_all.at[:, x, :, columns(k)]
         for side in sides:
-            send(part, part, side, grads_near[k])
+            send(part, part, side, normed_near[k])
 
     for copy in local[4 : N_LOCAL - 1]:
         copy.wait()
@@ -203,35 +232,58 @@
         far[i, :, half_columns[i]] = (
             far[i, :, half_columns[i]].astype(F32) + relay[i].astype(F32)
         ).astype(BF16)
+        pl.semaphore_wait(y_far[distance], 1)
         send(far.at[i], y_in.at[4 + i], y_device(distance), summed)
 
-    wait_bytes_of(normed_part(other_z, x, z_first), normed_crossed[z_first])
-    part = normed_part(other_z, x, z_first)
+    wait_bytes_of(grads_part(other_z, x, z_first), grads_crossed[z_first])
+    part = grads_part(other_z, x, z_first)
     crossed_near, crossed_far = receiver(), receiver()
     for side in sides:
         send(part, part, side, crossed_near)
     for k in chunks:
-        wait_bytes_of(normed_part(z, x_at[2], k), normed_far[k])
+        wait_bytes_of(grads_part(z, x_at[2], k), grads_far[k])
         if k != z_first:
-            part = normed_part(z, x_at[2], k)
-            send(part, part, across, normed_crossed[k])
+            part = grads_part(z, x_at[2], k)
+            send(part, part, across, grads_crossed[k])
     for k in chunks:
-        wait_bytes_of(grads_all.at[:, pl.ds(0, 2), :, columns(k)], grads_near[k])
-        part = grads_all.at[:, x_at[from_side(k % 2)], :, columns(k)]
-        send(part, part, sides[k % 2], grads_far[k])
+        wait_bytes_of(normed_all.at[:, pl.ds(0, 2), :, columns(k)], normed_near[k])
+        part = normed_all.at[:, x_at[from_side(k % 2)], :, columns(k)]
+        send(part, part, sides[k % 2], normed_far[k])
         if k == 1:
-            wait_bytes_of(normed_all.at[z, pl.ds(0, 2), :, columns(z_first)], crossed_near)
-            part = normed_part(other_z, x_at[from_side(z_first % 2)], z_first)
+            wait_bytes_of(grads_all.at[z, pl.ds(0, 2), :, columns(z_first)], crossed_near)
+            part = grads_part(other_z, x_at[from_side(z_first % 2)], z_first)
             send(part, part, sides[z_first % 2], crossed_far)
 
+    first = c == 0
+    exchanged, exchanged_grads, returned = receiver(), receiver(), receiver()
+
+    def blocks(ref, i, scale):
+        part = ref[:, i * HEAD_DIM : (i + 1) * HEAD_DIM] * scale
+        return part.reshape(8, ROWS, HEAD_DIM).astype(BF16)
+
+    def pick(pair, condition):
+        return jnp.where(condition, pair[0].astype(F32), pair[1].astype(F32)).astype(BF16)
+
+    def sequence(i):
+        return heads[i].astype(F32).reshape(SEQ, HEAD_DIM).astype(BF16)
+
+    acc_in[...] = jnp.zeros_like(acc_in)
     acc_back[...] = jnp.zeros_like(acc_back)
-    acc_in[...] = jnp.zeros_like(acc_in)
     for k in chunks:
-        wait_bytes_of(grads_all.at[:, x_at[2], :, columns(k)], grads_far[k])
-        acc_back[...] += lax.dot_general(
-            grads_all[:, :, :, columns(k)].reshape(HALF, GW), w_back[:, columns(k)],
-            CONTRACT_LAST, preferred_element_type=F32,
-        )
+        wait_bytes_of(normed_all.at[:, x_at[2], :, columns(k)], normed_far[k])
+        acc_in[...] += jnp.dot(
+            normed_all[:, :, :, columns(k)].reshape(HALF, GW), w_in[columns(k), :],
+            preferred_element_type=F32,
+        )
+    queries = [blocks(acc_in, i, width_scale) for i in range(2)]
+    heads_out[0] = pick(queries, ~first)
+    heads_out[1] = blocks(acc_in, 2, width_scale)
+    heads_out[2] = blocks(acc_in, 3, width_scale)
+    send(heads_out.at[pl.ds(0, 3)], heads.at[pl.ds(0, 3), :, c], sibling, exchanged)
+    heads[0, :, c] = pick(queries, first)
+    heads[1, :, c] = heads_out[1]
+    heads[2, :, c] = heads_out[2]
+
     wait_bytes_of(y_in, summed)
     total = w_back[y_rows(0, c * HEAD_DIM), :].astype(F32)
     for i in range(6):
@@ -263,6 +315,14 @@
     def line_sum(first, second):
         return (first.astype(F32) + second.astype(F32)).astype(BF16)
 
+    @pl.when(zh < Z_HI - 1)
+    def _():
+        pl.semaphore_wait(line_up, 1)
+
+    @pl.when(zh > 0)
+    def _():
+        pl.semaphore_wait(line_down, 1)
+
     @at(0)
     def _():
         line["up0"].start()
@@ -273,55 +333,35 @@
 
     for k in chunks:
         if k == z_first:
-            wait_bytes_of(normed_part(other_z, x_at[2], k), crossed_far)
+            wait_bytes_of(grads_part(other_z, x_at[2], k), crossed_far)
         else:
-            wait_bytes_of(normed_all.at[other_z, :, :, columns(k)], normed_crossed[k])
-        acc_in[...] += jnp.dot(
-            normed_all[:, :, :, columns(k)].reshape(HALF, GW), w_in[columns(k), :],
-            preferred_element_type=F32,
-        )
-
-    def blocks(value):
-        return value.reshape(8, ROWS, HEAD_DIM)
-
-    first = c == 0
-
-    def column_block(ref, i):
-        return ref[:, i * HEAD_DIM : (i + 1) * HEAD_DIM]
-
-    queries = [blocks(column_block(acc_in, i) * width_scale).astype(BF16) for i in range(2)]
-    head_grads = [blocks(column_block(acc_back, i) * out_scale).astype(BF16) for i in range(2)]
-    keyval = [blocks(column_block(acc_in, i) * width_scale).astype(BF16) for i in (2, 3)]
-
-    def pick(pair, condition):
-        return jnp.where(condition, pair[0].astype(F32), pair[1].astype(F32)).astype(BF16)
-
-    heads_out[0] = pick(queries, ~first)
-    heads_out[1] = pick(head_grads, ~first)
-    heads_out[2] = keyval[0]
-    heads_out[3] = keyval[1]
-    exchanged, returned = receiver(), receiver()
-    send(heads_out, heads.at[:, :, c], sibling, exchanged)
-    heads[0, :, c] = pick(queries, first)
-    heads[1, :, c] = pick(head_grads, first)
-    heads[2, :, c] = keyval[0]
-    heads[3, :, c] = keyval[1]
-    wait_bytes_of(heads_out, exchanged)
-
-    def sequence(i):
-        return heads[i].astype(F32).reshape(SEQ, HEAD_DIM).astype(BF16)
-
-    query, head_grad, key, value = [sequence(i) for i in range(4)]
-    key_parts, value_parts = [None] * 3, [None] * 3
-    for i in range(3):
-        limit = (i + 1) * 128
-        here = slice(i * 128, limit)
+            wait_bytes_of(grads_all.at[other_z, :, :, columns(k)], grads_crossed[k])
+        acc_back[...] += lax.dot_general(
+            grads_all[:, :, :, columns(k)].reshape(HALF, GW), w_back[:, columns(k)],
+            CONTRACT_LAST, preferred_element_type=F32,
+        )
+    head_grads = [blocks(acc_back, i, out_scale) for i in range(2)]
+    heads_out[3] = pick(head_grads, ~first)
+    send(heads_out.at[3], heads.at[3, :, c], sibling, exchanged_grads)
+    heads[3, :, c] = pick(head_grads, first)
+
+    wait_bytes_of(heads_out.at[pl.ds(0, 3)], exchanged)
+    query, key, value = [sequence(i) for i in range(3)]
+    row_blocks = [(slice(i * 128, (i + 1) * 128), (i + 1) * 128) for i in range(3)]
+    all_probs = []
+    for here, limit in row_blocks:
         scores = lax.dot_general(
             query[here], key[:limit], CONTRACT_LAST, preferred_element_type=F32
         )
         scores = scores * score_scale + bias[here, :limit]
         powers = jnp.exp(scores - jnp.max(scores, axis=-1, keepdims=True))
-        probs = powers / jnp.sum(powers, axis=-1, keepdims=True)
+        all_probs.append(powers / jnp.sum(powers, axis=-1, keepdims=True))
+
+    wait_bytes_of(heads_out.at[3], exchanged_grads)
+    head_grad = sequence(3)
+    key_parts, value_parts = [None] * 3, [None] * 3
+    for i, (here, limit) in enumerate(row_blocks):
+        probs = all_probs[i]
         prob_grads = lax.dot_general(
             head_grad[here], value[:limit], CONTRACT_LAST, preferred_element_type=F32
         )
@@ -331,8 +371,9 @@
             * score_scale
         ).astype(BF16)
         probs_low = probs.astype(BF16)
-        query_grads = jnp.dot(score_grads, key[:limit], preferred_element_type=F32)
-        grad_rows[0, here] = query_grads
+        grad_rows[0, here] = jnp.dot(
+            score_grads, key[:limit], preferred_element_type=F32
+        )
         for j in range(i + 1):
             there = slice(j * 128, (j + 1) * 128)
             key_term = lax.dot_general(
@@ -422,9 +463,9 @@
             terms[z, :, :, sum_columns(j)].astype(F32) + from_z_z[slot].astype(F32)
         ).astype(BF16)
         part = terms.at[z, x_at[2], :, sum_columns(j)]
-        send(part, hop_z.at[slot], sides[way], hopped[j], 4)
+        send(part, hop_z.at[slot], sides[way], hopped[j], 7)
         part = terms.at[z, x_at[forward_slot[1 - way]], :, sum_columns(j)]
-        send(part, near_z.at[slot, 0], sides[1 - way], neared[j], 4)
+        send(part, near_z.at[slot, 0], sides[1 - way], neared[j], 7)
 
     @at(2)
     def _():
@@ -454,7 +495,7 @@
             terms[z, x_at[forward], :, sum_columns(j)].astype(F32) + hop_z[slot].astype(F32)
         ).astype(BF16)
         part = terms.at[z, x_at[forward], :, sum_columns(j)]
-        send(part, near_z.at[slot, 1], sides[way], neared[j], 4)
+        send(part, near_z.at[slot, 1], sides[way], neared[j], 7)
 
     @at(0)
     def _():
@@ -501,9 +542,11 @@
     assert next(receivers, None) is None
     wait_bytes_of(w_in.at[pl.ds(0, 4368), :], send_sems.at[0])
     wait_bytes_of(all_weights, send_sems.at[1])
-    wait_bytes_of(terms.at[0, :, :, pl.ds(0, 7 * SW)], send_sems.at[4])
-    wait_bytes_of(terms.at[:, pl.ds(0, 3), :, pl.ds(0, 5 * SW)], send_sems.at[5])
-    wait_bytes_of(terms.at[0, 0, :, pl.ds(0, 5 * SW)], send_sems.at[6])
+    x_columns, z_columns = pl.ds(0, len(by_x) * SW), pl.ds(0, len(by_z) * SW)
+    wait_bytes_of(terms.at[0, :, :, z_columns], send_sems.at[4])
+    wait_bytes_of(terms.at[:, pl.ds(0, 3), :, x_columns], send_sems.at[5])
+    wait_bytes_of(terms.at[0, 0, :, x_columns], send_sems.at[6])
+    wait_bytes_of(terms.at[0, pl.ds(0, 3), :, z_columns], send_sems.at[7])
     for position, names in enumerate((("up0",), ("up1", "down1"), ("up2", "down2"), ("down3",))):
 
         @at(position)
@@ -588,6 +631,7 @@
             pltpu.SemaphoreType.DMA((N_SEND,)),
             pltpu.SemaphoreType.DMA((N_RECEIVE,)),
             pltpu.SemaphoreType.DMA((N_LOCAL,)),
+            pltpu.SemaphoreType.REGULAR((6,)),
         ],
         compiler_params=pltpu.CompilerParams(
             collective_id=0, has_side_effects=True, vmem_limit_bytes=63 * 2**20

time: 62.7 us -> 59.4 us (0.947)
  the two profiles are of different devices: /device:TPU:130 before, /device:TPU:256 now
where the time goes in v3:
time: 59.4 us; the launch traced here: 59.2 us
  Pallas kernels  58.6 us (99%)
  between operations  0.64 us (1%)
    pallas_call x1, Pallas kernels, on_device(): pl.pallas_call(kernel, out_shape=(jax.ShapeDtypeStruct((ROWS, D), BF16),...  56.9 us
    pallas_call x1, Pallas kernels, on_device(): pl.pallas_call(write_out, out_shape=(jax.ShapeDtypeStruct((1, ROWS, D), B...  1.72 us

profile of v3, /device:TPU:256, one launch (start us, length us, event | category | flops | bytes accessed | tf_op | source)
XLA Modules:
  0.0 59.2 jit_solution(12936496198435335740)
XLA Ops:
  0.6 56.9 %layer_backward.1 = (bf16[24,4608]{1,0:T(8,128)(2,1)}, f32[4,4608]{1,0:T(4,128)}, f32[4,4608]{1,0:T(4,128)}) custom-call(bf16[24,4608]{1,0:T(8,128)(2,1)} %bitcast.10, bf16[24,4608]{1,0:T(8,128)(2,1)} %bitcast.11, f32[4608]{0:T(1024)} %gain_hbm.1, s32[1,384]{1,0:T(1,128)} %docs_hbm.1, bf16[4608,128]{1,0:T(8,128)(2,1)} %bitcast.7, bf16[4608,128]{1,0:T(8,128)(2,1)} %bitcast.8, ...), custom_call_target="tpu_custom_call" | custom-call | tf_op jit(solution)/shard_map/layer_backward/pallas_call | solution.py:585
  57.5 1.7 %write_out.1 = (bf16[1,24,4608]{2,1,0:T(8,128)(2,1)}, f32[1,4,4608]{2,1,0:T(4,128)}, f32[1,4,4608]{2,1,0:T(4,128)}) custom-call(bf16[24,4608]{1,0:T(8,128)(2,1)} %get-tuple-element.6.first, f32[4,4608]{1,0:T(4,128)} %get-tuple-element.7.second, f32[4,4608]{1,0:T(4,128)} %get-tuple-element.8.third), custom_call_target="tpu_custom_call" | custom-call | tf_op jit(solution)/shard_map/write_out/pallas_call | solution.py:644

commit v4 on v3

--- a/solution.py
+++ b/solution.py
@@ -29,6 +29,9 @@
 SUM_PLAN = (
     ("z", 1), ("x", 0), ("z", 0), ("x", 1), ("z", 1), ("x", 0), ("x", 1), ("z", 0), ("x", 0), ("x", 1), ("x", 0), ("x", 1),
 )
+SUM_STEPS = (
+    (1, 1), (1, 3), (1, 0), (1, 5), (1, 6), (1, 2), (1, 8), (1, 9), (1, 4), (1, 10), (1, 11), (1, 7), (2, 1), (2, 3), (2, 0), (2, 5), (2, 6), (2, 2), (2, 8), (2, 9), (2, 4), (2, 10), (2, 11), (2, 7),
+)
 
 
 def kernel(
@@ -275,14 +278,27 @@
             normed_all[:, :, :, columns(k)].reshape(HALF, GW), w_in[columns(k), :],
             preferred_element_type=F32,
         )
-    queries = [blocks(acc_in, i, width_scale) for i in range(2)]
-    heads_out[0] = pick(queries, ~first)
-    heads_out[1] = blocks(acc_in, 2, width_scale)
-    heads_out[2] = blocks(acc_in, 3, width_scale)
-    send(heads_out.at[pl.ds(0, 3)], heads.at[pl.ds(0, 3), :, c], sibling, exchanged)
+        if k == GATHER - 1:
+            queries = [blocks(acc_in, i, width_scale) for i in range(2)]
+            heads_out[0] = pick(queries, ~first)
+            heads_out[1] = blocks(acc_in, 2, width_scale)
+            heads_out[2] = blocks(acc_in, 3, width_scale)
+            send(heads_out.at[pl.ds(0, 3)], heads.at[pl.ds(0, 3), :, c], sibling, exchanged)
+        if k == z_first:
+            wait_bytes_of(grads_part(other_z, x_at[2], k), crossed_far)
+        else:
+            wait_bytes_of(grads_all.at[other_z, :, :, columns(k)], grads_crossed[k])
+        acc_back[...] += lax.dot_general(
+            grads_all[:, :, :, columns(k)].reshape(HALF, GW), w_back[:, columns(k)],
+            CONTRACT_LAST, preferred_element_type=F32,
+        )
+    head_grads = [blocks(acc_back, i, out_scale) for i in range(2)]
+    heads_out[3] = pick(head_grads, ~first)
+    send(heads_out.at[3], heads.at[3, :, c], sibling, exchanged_grads)
     heads[0, :, c] = pick(queries, first)
     heads[1, :, c] = heads_out[1]
     heads[2, :, c] = heads_out[2]
+    heads[3, :, c] = pick(head_grads, first)
 
     wait_bytes_of(y_in, summed)
     total = w_back[y_rows(0, c * HEAD_DIM), :].astype(F32)
@@ -330,20 +346,6 @@
     @at(3)
     def _():
         line["down3"].start()
-
-    for k in chunks:
-        if k == z_first:
-            wait_bytes_of(grads_part(other_z, x_at[2], k), crossed_far)
-        else:
-            wait_bytes_of(grads_all.at[other_z, :, :, columns(k)], grads_crossed[k])
-        acc_back[...] += lax.dot_general(
-            grads_all[:, :, :, columns(k)].reshape(HALF, GW), w_back[:, columns(k)],
-            CONTRACT_LAST, preferred_element_type=F32,
-        )
-    head_grads = [blocks(acc_back, i, out_scale) for i in range(2)]
-    heads_out[3] = pick(head_grads, ~first)
-    send(heads_out.at[3], heads.at[3, :, c], sibling, exchanged_grads)
-    heads[3, :, c] = pick(head_grads, first)
 
     wait_bytes_of(heads_out.at[pl.ds(0, 3)], exchanged)
     query, key, value = [sequence(i) for i in range(3)]
@@ -449,53 +451,62 @@
             part = terms.at[:, x_at[forward_slot[1 - way]], :, sum_columns(j)]
             send(part, near_x.at[slot, 0], sides[1 - way], neared[j], 5)
 
-    for slot, (j, way) in enumerate(by_x):
-        forward = forward_slot[way]
-        wait_bytes_of(hop_x.at[slot], hopped[j])
-        terms[:, x_at[forward], :, sum_columns(j)] = (
-            terms[:, x_at[forward], :, sum_columns(j)].astype(F32) + hop_x[slot].astype(F32)
-        ).astype(BF16)
-        part = terms.at[:, x_at[forward], :, sum_columns(j)]
-        send(part, near_x.at[slot, 1], sides[way], neared[j], 5)
-    for slot, (j, way) in enumerate(by_z):
-        wait_bytes_of(from_z_z.at[slot], crossed[j])
-        terms[z, :, :, sum_columns(j)] = (
-            terms[z, :, :, sum_columns(j)].astype(F32) + from_z_z[slot].astype(F32)
-        ).astype(BF16)
-        part = terms.at[z, x_at[2], :, sum_columns(j)]
-        send(part, hop_z.at[slot], sides[way], hopped[j], 7)
-        part = terms.at[z, x_at[forward_slot[1 - way]], :, sum_columns(j)]
-        send(part, near_z.at[slot, 0], sides[1 - way], neared[j], 7)
-
-    @at(2)
-    def _():
-        line["up1"].wait_recv()
-        up_out[2:3] = line_sum(z_out[3:4], up_in[2:3])
-        line["up2"].start()
-
-    @at(1)
-    def _():
-        line["down2"].wait_recv()
-        down_out[2:3] = line_sum(z_out[0:1], down_in[0:1])
-        line["down1"].start()
-
-    for slot, (j, way) in enumerate(by_x):
-        wait_bytes_of(near_x.at[slot], neared[j])
-        terms[:, x, :, sum_columns(j)] = (
-            terms[:, x, :, sum_columns(j)].astype(F32)
-            + near_x[slot, 0].astype(F32)
-            + near_x[slot, 1].astype(F32)
-        ).astype(BF16)
-        part = terms.at[other_z, x, :, sum_columns(j)]
-        send(part, from_z_x.at[slot], across, crossed[j], 6)
-    for slot, (j, way) in enumerate(by_z):
-        forward = forward_slot[way]
-        wait_bytes_of(hop_z.at[slot], hopped[j])
-        terms[z, x_at[forward], :, sum_columns(j)] = (
-            terms[z, x_at[forward], :, sum_columns(j)].astype(F32) + hop_z[slot].astype(F32)
-        ).astype(BF16)
-        part = terms.at[z, x_at[forward], :, sum_columns(j)]
-        send(part, near_z.at[slot, 1], sides[way], neared[j], 7)
+    def line_end():
+        @at(2)
+        def _():
+            line["up1"].wait_recv()
+            up_out[2:3] = line_sum(z_out[3:4], up_in[2:3])
+            line["up2"].start()
+
+        @at(1)
+        def _():
+            line["down2"].wait_recv()
+            down_out[2:3] = line_sum(z_out[0:1], down_in[0:1])
+            line["down1"].start()
+
+    def over_x(j, way, stage):
+        slot, forward = slot_of[j], x_at[forward_slot[way]]
+        if stage == 1:
+            wait_bytes_of(hop_x.at[slot], hopped[j])
+            terms[:, forward, :, sum_columns(j)] = (
+                terms[:, forward, :, sum_columns(j)].astype(F32) + hop_x[slot].astype(F32)
+            ).astype(BF16)
+            part = terms.at[:, forward, :, sum_columns(j)]
+            send(part, near_x.at[slot, 1], sides[way], neared[j], 5)
+        else:
+            wait_bytes_of(near_x.at[slot], neared[j])
+            terms[:, x, :, sum_columns(j)] = (
+                terms[:, x, :, sum_columns(j)].astype(F32)
+                + near_x[slot, 0].astype(F32)
+                + near_x[slot, 1].astype(F32)
+            ).astype(BF16)
+            part = terms.at[other_z, x, :, sum_columns(j)]
+            send(part, from_z_x.at[slot], across, crossed[j], 6)
+
+    def over_z(j, way, stage):
+        slot, forward = slot_of[j], x_at[forward_slot[way]]
+        if stage == 1:
+            wait_bytes_of(from_z_z.at[slot], crossed[j])
+            terms[z, :, :, sum_columns(j)] = (
+                terms[z, :, :, sum_columns(j)].astype(F32) + from_z_z[slot].astype(F32)
+            ).astype(BF16)
+            part = terms.at[z, x_at[2], :, sum_columns(j)]
+            send(part, hop_z.at[slot], sides[way], hopped[j], 7)
+            part = terms.at[z, x_at[forward_slot[1 - way]], :, sum_columns(j)]
+            send(part, near_z.at[slot, 0], sides[1 - way], neared[j], 7)
+        else:
+            wait_bytes_of(hop_z.at[slot], hopped[j])
+            terms[z, forward, :, sum_columns(j)] = (
+                terms[z, forward, :, sum_columns(j)].astype(F32) + hop_z[slot].astype(F32)
+            ).astype(BF16)
+            part = terms.at[z, forward, :, sum_columns(j)]
+            send(part, near_z.at[slot, 1], sides[way], neared[j], 7)
+
+    for place, (stage, j) in enumerate(SUM_STEPS):
+        if place == len(SUM_STEPS) // 2:
+            line_end()
+        kind, way = SUM_PLAN[j]
+        (over_x if kind == "x" else over_z)(j, way, stage)
 
     @at(0)
     def _():

time: 59.4 us -> 58.4 us (0.983)
  the two profiles are of different devices: /device:TPU:256 before, /device:TPU:8 now
where the time goes in v4:
time: 58.4 us; the launch traced here: 58.3 us
  Pallas kernels  57.6 us (99%)
  between operations  0.64 us (1%)
    pallas_call x1, Pallas kernels, on_device(): pl.pallas_call(kernel, out_shape=(jax.ShapeDtypeStruct((ROWS, D), BF16),...  55.9 us
    pallas_call x1, Pallas kernels, on_device(): pl.pallas_call(write_out, out_shape=(jax.ShapeDtypeStruct((1, ROWS, D), B...  1.72 us

profile of v4, /device:TPU:8, one launch (start us, length us, event | category | flops | bytes accessed | tf_op | source)
XLA Modules:
  0.0 58.3 jit_solution(4058482410073420822)
XLA Ops:
  0.6 55.9 %layer_backward.1 = (bf16[24,4608]{1,0:T(8,128)(2,1)}, f32[4,4608]{1,0:T(4,128)}, f32[4,4608]{1,0:T(4,128)}) custom-call(bf16[24,4608]{1,0:T(8,128)(2,1)} %bitcast.10, bf16[24,4608]{1,0:T(8,128)(2,1)} %bitcast.11, f32[4608]{0:T(1024)} %gain_hbm.1, s32[1,384]{1,0:T(1,128)} %docs_hbm.1, bf16[4608,128]{1,0:T(8,128)(2,1)} %bitcast.7, bf16[4608,128]{1,0:T(8,128)(2,1)} %bitcast.8, ...), custom_call_target="tpu_custom_call" | custom-call | tf_op jit(solution)/shard_map/layer_backward/pallas_call | solution.py:596
  56.6 1.7 %write_out.1 = (bf16[1,24,4608]{2,1,0:T(8,128)(2,1)}, f32[1,4,4608]{2,1,0:T(4,128)}, f32[1,4,4608]{2,1,0:T(4,128)}) custom-call(bf16[24,4608]{1,0:T(8,128)(2,1)} %get-tuple-element.6.first, f32[4,4608]{1,0:T(4,128)} %get-tuple-element.7.second, f32[4,4608]{1,0:T(4,128)} %get-tuple-element.8.third), custom_call_target="tpu_custom_call" | custom-call | tf_op jit(solution)/shard_map/write_out/pallas_call | solution.py:655
